TPU v7x, 32 devices: a whole 2x2x4 slice. The times are simulated.
32 devices in a mesh: dp: 4 (over y, x), ctx: 8 (over z, core).
Axes of the slice: x: 2, y: 2, z: 4, core: 2. Of those that a mesh axis runs over, the one named last changes fastest.
Arguments:
- tokens: bfloat16 [4, 4096, 960], P('dp', 'ctx'), may hold values from -6 to 6
- positions: int32 [4, 4096], P('dp', 'ctx'), may hold values from 0 to 4095, as said below
- w_qkv: bfloat16 [960, 1600], P('dp'), may hold values from -0.12909944 to 0.12909944
- w_out: bfloat16 [960, 960], P('dp'), may hold values from -3 to 3
- w_gate: bfloat16 [960, 2560], P('dp'), may hold values from -0.1875 to 0.1875
- w_up: bfloat16 [960, 2560], P('dp'), may hold values from -0.1875 to 0.1875
- w_down: bfloat16 [2560, 960], P('dp'), may hold values from -0.125 to 0.125
- g_attn: bfloat16 [960], P('dp'), may hold values from 0.5 to 1.5
- g_mlp: bfloat16 [960], P('dp'), may hold values from 0.5 to 1.5
- grad_out: bfloat16 [4, 4096, 960], P('dp', 'ctx'), may hold values from -6 to 6
Outputs:
- output: bfloat16 [4, 4096, 960], P('dp', 'ctx')
- grad_tokens: bfloat16 [4, 4096, 960], P('dp', 'ctx')
- grad_qkv: float32 [960, 1600], P('dp')
- grad_wo: float32 [960, 960], P('dp')
- grad_gate: float32 [960, 2560], P('dp')
- grad_up: float32 [960, 2560], P('dp')
- grad_down: float32 [2560, 960], P('dp')
- grad_g_attn: float32 [960], P('dp')
- grad_g_mlp: float32 [960], P('dp')
Inputs may be any that keep to these rules, and one draw needn't show every extreme that they name: In each sequence positions are a permutation of 0 to 4095: stored tokens in rows r * 512 to (r + 1) * 512 - 1 hold two runs of 256 consecutive positions in rising order, position blocks b and 15 - b of 256 positions each, with b differing from r to r.
All inputs are finite; a program needn't handle non-finite values.
Results may differ from a plain program's by a relative error of at most 0.023.
Values may be sent and summed in bfloat16 or wider, within the bound.
No kernel may reach another device: no remote copies, remote signals or barrier semaphores. Data moves between devices by JAX's collectives and lax.ppermute only.
A program may use at most 256 MiB of HBM per device.

v0:
```python
import functools

import jax
import jax.numpy as jnp
from jax import lax
from jax.experimental import pallas as pl
from jax.experimental.pallas import tpu as pltpu
from jax.sharding import PartitionSpec as P

QUERY_HEADS = 15
KEY_VALUE_HEADS = 5
HEAD_SIZE = 64
GROUPS = QUERY_HEADS // KEY_VALUE_HEADS
QW = QUERY_HEADS * HEAD_SIZE
KW = KEY_VALUE_HEADS * HEAD_SIZE
EPS = 1e-05
THETA = 10000.0
MASK_FILL = -1e30
F32 = jnp.float32
BF16 = jnp.bfloat16
NT = (((1,), (1,)), ((), ()))
CORES = 2
SWAP_ROWS = 16
MIB = 2**20


def dot(a, b):
    return jnp.dot(a, b, preferred_element_type=F32)


def dot_nt(a, b):
    return lax.dot_general(a, b, NT, preferred_element_type=F32)


def call(kernel, name, outs, args, smem=0, scratch=(), limit=32, us=10, aliases=None):
    specs = [pl.BlockSpec(memory_space=pltpu.SMEM)] * smem
    specs += [pl.BlockSpec(memory_space=pltpu.VMEM)] * (len(args) - smem)
    return pl.pallas_call(
        kernel,
        out_shape=tuple(jax.ShapeDtypeStruct(s, d) for s, d in outs),
        in_specs=specs,
        out_specs=tuple(pl.BlockSpec(memory_space=pltpu.VMEM) for _ in outs),
        scratch_shapes=list(scratch),
        compiler_params=pltpu.CompilerParams(vmem_limit_bytes=limit * MIB),
        cost_estimate=pl.CostEstimate(
            flops=int(us * 1e7), bytes_accessed=0, transcendentals=0
        ),
        input_output_aliases=aliases or {},
        name=name,
    )(*args)


class Plan:
    def __init__(self, nd, nc):
        self.nd, self.nz = nd, nc // CORES
        self.kd, self.kz = nd.bit_length() - 1, self.nz.bit_length() - 1
        self.core = lax.axis_index("ctx") % CORES
        self.z = lax.axis_index("ctx") // CORES
        self.d = lax.axis_index("dp")
        self.gates = ()

    def order(self, k, core):
        return [(j + core) % k for j in range(k)]

    def masks(self, k, core):
        order = self.order(k, core)
        return [
            sum(1 << order[j] for j in range(k) if (p >> j) & 1) for p in range(1 << k)
        ]

    def place(self, d, z, c):
        return (d * self.nz + z) * CORES + c

    def everywhere(self):
        for d in range(self.nd):
            for z in range(self.nz):
                for c in range(CORES):
                    yield d, z, c

    def hop_d(self, x, j):
        perm = [
            (
                self.place(d, z, c),
                self.place(d ^ (1 << self.order(self.kd, c)[j]), z, c),
            )
            for d, z, c in self.everywhere()
        ]
        return lax.ppermute(after(x, *self.gates), ("dp", "ctx"), perm)

    def hop_z(self, x, j):
        perm = [
            (
                self.place(d, z, c),
                self.place(d, z ^ (1 << self.order(self.kz, c)[j]), c),
            )
            for d, z, c in self.everywhere()
        ]
        return lax.ppermute(after(x, *self.gates), ("dp", "ctx"), perm)

    def swap(self, x):
        perm = [(self.place(d, z, c), self.place(d, z, 1 - c)) for d, z, c in self.everywhere()]
        return lax.ppermute(after(x, *self.gates), ("dp", "ctx"), perm)

    def spread(self, x, k, hop):
        held = [x]
        for j in range(k):
            for h in list(held):
                held.append(hop(h, j))
                yield held[-1]
        return held

    def fold(self, near, far, k, hop):
        terms = [near]
        for j in reversed(range(k)):
            got = hop(far, j)
            yield got
            got = after(got, *self.gates)
            terms.append(got)
            if j:
                half = got.shape[0] // 2
                far = add(*[t[half:] for t in terms])
                terms = [t[:half] for t in terms]
        return add(*terms)

    def double_z(self, x):
        for j in range(self.kz):
            got = self.hop_z(x, j)
            yield got
            x = add(x, got)
        return x

    def owners(self):
        m0 = jnp.array(self.masks(self.kd, 0), jnp.int32)
        m1 = jnp.array(self.masks(self.kd, 1), jnp.int32)
        mine = jnp.where(self.core == 0, m0, m1) ^ self.d
        other = jnp.where(self.core == 0, m1, m0) ^ self.d
        return jnp.concatenate([self.core[None], mine, other]).astype(jnp.int32)

    def total_z(self, x):
        sizes = []
        for j in reversed(range(self.kz)):
            order = jnp.where(
                self.core == 0, self.order(self.kz, 0)[j], self.order(self.kz, 1)[j]
            )
            bit = (self.z >> order) & 1
            rows = x.shape[0]
            size = -(-rows // 16) * 8
            keep = lax.dynamic_slice_in_dim(x, bit * (rows - size), size, 0)
            send = lax.dynamic_slice_in_dim(x, (1 - bit) * (rows - size), size, 0)
            sizes.append((bit, rows, size))
            got = self.hop_z(send, j)
            yield got
            got = after(got, *self.gates)
            x = add(keep, got)
        for j in range(self.kz):
            bit, rows, size = sizes.pop()
            got = self.hop_z(x, j)
            yield got
            low = jnp.where(bit == 0, x, got)
            high = jnp.where(bit == 0, got, x)
            x = jnp.concatenate([low[: rows - size], high], axis=0)
        return x

    def reduce_all(self, near, far, small=False):
        x = yield from self.fold(near, far, self.kd, self.hop_d)
        x = yield from (self.double_z if small else self.total_z)(x)
        other = self.swap(x)
        yield other
        return jnp.where(self.core == 0, x, other), jnp.where(self.core == 0, other, x)


class Task:
    def __init__(self, steps):
        self.steps, self.out, self.done, self.result = steps, [], False, None

    def go(self, n=1000):
        while n > 0 and not self.done:
            try:
                self.out.append(next(self.steps))
            except StopIteration as stop:
                self.done, self.result = True, stop.value
            n -= 1
        return self

    def finish(self):
        return self.go().result


def settle(outs, *tasks):
    waited = []
    for task in tasks:
        if isinstance(task, Task):
            waited += task.out
            task.out = []
        else:
            waited.append(task)
    if not waited:
        return tuple(outs)
    return lax.optimization_barrier((*outs, *waited))[: len(outs)]


def after(x, *tasks):
    return settle((x,), *tasks)[0]


def add(*terms):
    if len(terms) == 1:
        return terms[0]
    return functools.reduce(lambda a, b: a + b, [t.astype(F32) for t in terms]).astype(BF16)


def row_split(rows):
    offset = rows // 2 // 16 * 16
    return offset, rows - offset


def start_row(idx, slot, parity, rows, offset):
    return pl.multiple_of(idx[slot] * rows + parity * offset, 8)


def pack_kernel(nd, idx, gate, up, down_t, w_out, pack):
    rows, width = gate.shape[0], pack.shape[1]
    down = down_t[...].T
    shard, model = down.shape
    quarter = shard // 4
    rest, half = model - width, quarter // 2
    for core in range(CORES):

        @pl.when(idx[0] == core)
        def _(core=core):
            for f in range(2):
                at = core * 2 * quarter + f * quarter
                out = pack.at[pl.ds(f * (2 * rows + quarter + half), 2 * rows + quarter + half)]
                for j in range(nd):
                    src = slice(j * shard + at, j * shard + at + quarter)
                    dst = slice(j * quarter, (j + 1) * quarter)
                    out[0:rows, dst] = gate[:, src]
                    out[rows : 2 * rows, dst] = up[:, src]
                block = down[at : at + quarter, :]
                tail = 2 * rows + quarter
                out[2 * rows : tail, :] = block[:, :width]
                out[tail : tail + half, 0:rest] = block[:half, width:]
                out[tail : tail + half, rest:] = block[half:, width:]

    end = pack.shape[0] - rows - rows // 2
    half = rows // 2
    pack[end : end + rows, :] = w_out[:, :width]
    pack[end + rows :, 0:rest] = w_out[0:half, width:]
    pack[end + rows :, rest:] = w_out[half:, width:]


def gain_column(gain_ref, which):
    lane = (QW + 2 * KW) % 128 + which
    return gain_ref[...].astype(F32)[:, lane : lane + 1]


def project_kernel(nd, idx, pos, cos, sin, x_ref, *refs):
    pieces = refs[: 2 * nd]
    normed_ref, q_ref, kv_ref, w_ref, gain_ref = refs[2 * nd :]
    model = x_ref.shape[0]
    rows = model // nd
    offset, take = row_split(rows)
    core = idx[0]
    for p in range(nd):
        w_ref[pl.ds(start_row(idx, 1 + p, core, rows, offset), take), :] = pieces[p][...]
        w_ref[pl.ds(start_row(idx, 1 + nd + p, 1 - core, rows, offset), take), :] = pieces[
            nd + p
        ][...]
    low = (QW + 2 * KW) // 128 * 128
    gain_ref[...] = w_ref[:, low : low + 128]
    x = x_ref[...].astype(F32)
    factor = lax.rsqrt(jnp.mean(x * x, axis=0, keepdims=True) + EPS)
    normed = (x * factor * gain_column(gain_ref, 0)).astype(BF16)
    normed_ref[...] = normed
    normed = normed.T
    half = HEAD_SIZE // 2
    c, s = cos[...], sin[...]
    heads = 10
    for b in range(0, w_ref.shape[1], heads * HEAD_SIZE):
        block = dot(normed, w_ref[:, b : b + heads * HEAD_SIZE]).T
        for i in range(heads):
            head = b // HEAD_SIZE + i
            if head >= QUERY_HEADS + 2 * KEY_VALUE_HEADS:
                break
            u1 = block[i * HEAD_SIZE : i * HEAD_SIZE + half]
            u2 = block[i * HEAD_SIZE + half : (i + 1) * HEAD_SIZE]
            if head < QUERY_HEADS + KEY_VALUE_HEADS:
                u1, u2 = u1 * c - u2 * s, u2 * c + u1 * s
            both = jnp.concatenate([u1, u2], axis=0).astype(BF16)
            if head < QUERY_HEADS:
                q_ref[head * HEAD_SIZE : (head + 1) * HEAD_SIZE] = (
                    both.astype(F32) * HEAD_SIZE**-0.5
                ).astype(BF16)
            else:
                at = (head - QUERY_HEADS) * HEAD_SIZE
                kv_ref[at : at + HEAD_SIZE] = both
    run = x_ref.shape[1] // 2
    blocks = jnp.broadcast_to(
        (pos[...] // run).astype(F32), (kv_ref.shape[0] - 2 * KW, x_ref.shape[1])
    )
    kv_ref[2 * KW :, :] = blocks.astype(BF16)


def list_pairs(q_blocks, kv_s, count, run, todo):
    n = jnp.int32(0)
    for rank in range(count):
        for part in range(2):
            tile = kv_s[rank, 2 * KW : 2 * KW + 16, part * run : part * run + 128]
            block = jnp.max(tile.astype(F32)).astype(jnp.int32)
            for r in range(2):
                active = block < q_blocks[r]

                @pl.when(active)
                def _(n=n, code=r * 256 + rank * 2 + part):
                    todo[n] = code

                n = n + active.astype(jnp.int32)
    return n


def each_pair(todo, n, run, pair):
    def body(i, _):
        code = todo[i]
        r = code // 256
        block = code % 256
        pair(
            block // 2,
            pl.multiple_of((block % 2) * run, run),
            pl.multiple_of(r * run, run),
            False,
        )
        return 0

    lax.fori_loop(0, n, body, 0)


def forward_kernel(count, first, last, run, q_blocks, qT, *refs):
    kvs, refs = refs[:count], refs[count:]
    if not first:
        m_in, l_in, acc_in = refs[:3]
        refs = refs[3:]
    if last:
        o_ref, lse_ref, kv_s, m_s, l_s, acc_s, todo = refs
    else:
        m_s, l_s, acc_s, kv_s, todo = refs
    for i in range(count):
        kv_s[i] = kvs[i][...]
    if not first:
        m_s[...] = m_in[...]
        l_s[...] = l_in[...]
        acc_s[...] = acc_in[...]
    n = list_pairs(q_blocks, kv_s, count, run, todo)
    keep = lax.broadcasted_iota(jnp.int32, (run, run), 0) <= lax.broadcasted_iota(
        jnp.int32, (run, run), 1
    )

    def pair(rank, ko, qo, diag):
        def scores(hd):
            h = hd // GROUPS
            k = kv_s[rank, h * HEAD_SIZE : (h + 1) * HEAD_SIZE, pl.ds(ko, run)].T
            return dot(k, qT[hd * HEAD_SIZE : (hd + 1) * HEAD_SIZE, pl.ds(qo, run)])

        def flush(hd, p, shrink):
            h = KEY_VALUE_HEADS + hd // GROUPS
            vT = kv_s[rank, h * HEAD_SIZE : (h + 1) * HEAD_SIZE, pl.ds(ko, run)]
            o = dot(vT, p)
            rows = slice(hd * HEAD_SIZE, (hd + 1) * HEAD_SIZE)
            if shrink is not None:
                o = acc_s[rows, pl.ds(qo, run)] * shrink + o
            acc_s[rows, pl.ds(qo, run)] = o

        if not diag:
            m_all = m_s[:, pl.ds(qo, run)]
            l_all = l_s[:, pl.ds(qo, run)]

        def top(hd, s):
            if diag:
                s = jnp.where(keep, s, MASK_FILL)
            m = jnp.max(s, axis=0, keepdims=True)
            if not diag:
                m = jnp.maximum(m_all[hd : hd + 1], m)
            return s, m

        ms, ls, pending = [], [], None
        current = top(0, scores(0))
        following = scores(1)
        for hd in range(QUERY_HEADS):
            s, m = current
            if hd + 1 < QUERY_HEADS:
                current = top(hd + 1, following)
            if hd + 2 < QUERY_HEADS:
                following = scores(hd + 2)
            if pending is not None:
                flush(*pending)
            p = jnp.exp(s - m)
            total = jnp.sum(p, axis=0, keepdims=True)
            shrink = None
            if not diag:
                shrink = jnp.exp(m_all[hd : hd + 1] - m)
                total = l_all[hd : hd + 1] * shrink + total
            ms.append(m)
            ls.append(total)
            pending = (hd, p.astype(BF16), shrink)
        flush(*pending)
        m_s[:, pl.ds(qo, run)] = jnp.concatenate(ms + ms[-1:], 0)
        l_s[:, pl.ds(qo, run)] = jnp.concatenate(ls + ls[-1:], 0)

    if first:
        for r in range(2):
            pair(0, r * run, r * run, True)
    each_pair(todo, n, run, pair)
    if last:
        lse_ref[...] = m_s[...] + jnp.log(l_s[...])
        for hd in range(QUERY_HEADS):
            rows = slice(hd * HEAD_SIZE, (hd + 1) * HEAD_SIZE)
            o_ref[rows, :] = (acc_s[rows, :] / l_s[hd : hd + 1, :]).astype(BF16)


def forward_wave(q_blocks, qT, kvs, state, last, us):
    tokens = qT.shape[1]
    stats = pltpu.VMEM((16, tokens), F32)
    kv_s = pltpu.VMEM((len(kvs),) + kvs[0].shape, BF16)
    todo = pltpu.SMEM((4 * len(kvs),), jnp.int32)
    first = state is None
    args = [q_blocks, qT] + list(kvs) + ([] if first else list(state))
    if last:
        outs = [((QW, tokens), BF16), ((16, tokens), F32)]
        scratch = [kv_s, stats, stats, pltpu.VMEM((QW, tokens), F32), todo]
    else:
        outs = [((16, tokens), F32), ((16, tokens), F32), ((QW, tokens), F32)]
        scratch = [kv_s, todo]
    return call(
        functools.partial(forward_kernel, len(kvs), first, last, tokens // 2),
        "attention_forward",
        outs,
        args,
        smem=1,
        scratch=scratch,
        limit=12 + 2 * len(kvs),
        us=us,
    )


def backward_kernel(first, last, terms, run, q_blocks, *refs):
    q_own, q_sib, do_own, do_sib, st_own, st_sib, kv = refs[:7]
    before, refs = refs[7 : 7 + terms], refs[7 + terms :]
    if not first:
        dq_in, refs = refs[0], refs[1:]
    if last:
        dq_own, dq_sib, out, dq_s, q_s, do_s, st_s, dkv_s, todo = refs
    else:
        dq_s, out, q_s, do_s, st_s, dkv_s, todo = refs
    for s, (q, do, st) in enumerate(((q_own, do_own, st_own), (q_sib, do_sib, st_sib))):
        q_s[s] = q[...]
        do_s[s] = do[...]
        st_s[s] = st[...]
    if terms:
        dkv_s[...] = functools.reduce(lambda a, b: a + b, [t[...].astype(F32) for t in before])
    else:
        dkv_s[...] = jnp.zeros_like(dkv_s)
    dq_s[...] = jnp.zeros_like(dq_s) if first else dq_in[...]
    n = jnp.int32(0)
    for part in range(2):
        tile = kv[2 * KW : 2 * KW + 16, part * run : part * run + 128]
        block = jnp.max(tile.astype(F32)).astype(jnp.int32)
        for r in range(4):
            active = block < q_blocks[r]

            @pl.when(active)
            def _(n=n, code=r * 2 + part):
                todo[n] = code

            n = n + active.astype(jnp.int32)
    keep = lax.broadcasted_iota(jnp.int32, (run, run), 0) <= lax.broadcasted_iota(
        jnp.int32, (run, run), 1
    )

    def pair(who, ko, qo, diag):
        lse_all = st_s[who, 0:16, pl.ds(qo, run)]
        delta_all = st_s[who, 16:32, pl.ds(qo, run)]

        def rows(h):
            return slice(h * HEAD_SIZE, (h + 1) * HEAD_SIZE)

        def opening(hd):
            h = hd // GROUPS
            k = kv[rows(h), pl.ds(ko, run)].T
            v = kv[rows(KEY_VALUE_HEADS + h), pl.ds(ko, run)].T
            return (
                dot(k, q_s[who, rows(hd), pl.ds(qo, run)]),
                dot(v, do_s[who, rows(hd), pl.ds(qo, run)]),
            )

        def closing(hd, p, ds):
            h = hd // GROUPS
            q = q_s[who, rows(hd), pl.ds(qo, run)]
            do = do_s[who, rows(hd), pl.ds(qo, run)]
            kT = kv[rows(h), pl.ds(ko, run)]
            dkv_s[rows(KEY_VALUE_HEADS + h), pl.ds(ko, run)] += dot_nt(do, p)
            dkv_s[rows(h), pl.ds(ko, run)] += dot_nt(q, ds)
            dq_s[who, rows(hd), pl.ds(qo, run)] += dot(kT, ds)

        following, pending = opening(0), None
        for hd in range(QUERY_HEADS):
            s, dp = following
            if hd + 1 < QUERY_HEADS:
                following = opening(hd + 1)
            if pending is not None:
                closing(*pending)
            p = jnp.exp(s - lse_all[hd : hd + 1])
            if diag:
                p = jnp.where(keep, p, 0.0)
            ds = (p * (dp - delta_all[hd : hd + 1])).astype(BF16)
            pending = (hd, p.astype(BF16), ds)
        closing(*pending)

    if last:
        for r in range(2):
            pair(0, r * run, r * run, True)

    def body(i, _):
        code = todo[i]
        r = code // 2
        pair(
            r // 2,
            pl.multiple_of((code % 2) * run, run),
            pl.multiple_of((r % 2) * run, run),
            False,
        )
        return 0

    lax.fori_loop(0, n, body, 0)
    out[...] = dkv_s[...].astype(BF16)
    if last:
        dq_own[...] = dq_s[0]
        dq_sib[...] = dq_s[1].astype(BF16)


def backward_wave(q_blocks, qs, dos, stats, kv, before, dq, last, us):
    tokens = kv.shape[1]
    both = (2, QW, tokens)
    args = [q_blocks, *qs, *dos, *stats, kv, *before] + ([] if dq is None else [dq])
    scratch = [
        pltpu.VMEM(both, BF16),
        pltpu.VMEM(both, BF16),
        pltpu.VMEM((2, 32, tokens), F32),
        pltpu.VMEM((2 * KW, tokens), F32),
        pltpu.SMEM((16,), jnp.int32),
    ]
    out = ((2 * KW, tokens), BF16)
    if last:
        outs = [((QW, tokens), F32), ((QW, tokens), BF16), out]
        scratch = [pltpu.VMEM(both, F32)] + scratch
    else:
        outs = [(both, F32), out]
    return call(
        functools.partial(backward_kernel, dq is None, last, len(before), tokens // 2),
        "attention_backward",
        outs,
        args,
        smem=1,
        scratch=scratch,
        limit=28,
        us=us,
    )


def middle_kernel(nd, idx, x_ref, oT, gain_ref, *refs):
    pieces = refs[:nd]
    mid_ref, normed_ref, w_ref = refs[nd:]
    rows, width = w_ref.shape[0] // nd, pieces[0].shape[1]
    rest, half = w_ref.shape[1] - width, rows // 2
    end = pieces[0].shape[0] - rows - half
    for p in range(nd):
        at = pl.multiple_of(idx[1 + p] * rows, 8)
        w_ref[pl.ds(at, rows), 0:width] = pieces[p][end : end + rows]
        w_ref[pl.ds(at, half), width:] = pieces[p][end + rows :, 0:rest]
        w_ref[pl.ds(pl.multiple_of(at + half, 8), half), width:] = pieces[p][end + rows :, rest:]
    mid = x_ref[...].astype(F32) + dot(w_ref[...].T, oT[...])
    mid_ref[...] = mid
    factor = lax.rsqrt(jnp.mean(mid * mid, axis=0, keepdims=True) + EPS)
    normed_ref[...] = (mid * factor * gain_column(gain_ref, 1)).astype(BF16)


def mlp_kernel(nd, idx, n_own, n_sib, dy_own, dy_sib, *refs):
    pieces, sums, stacks = refs[:nd], refs[nd : nd + 4], refs[nd + 4 : nd + 6]
    wg, wu, wd, wgT, wuT, wdT, nT, dyT, actT, dg_s, du_s = refs[nd + 6 :]
    model = wg.shape[0]
    rows, quarter, width = model // nd, wd.shape[0] // nd, wd.shape[0]
    half, rest, tail = quarter // 2, model - width, 2 * rows + quarter
    size = tail + half
    tokens = n_own.shape[1]
    nT[:, 0:tokens] = n_own[...]
    nT[:, tokens:] = n_sib[...]
    dyT[:, 0:tokens] = dy_own[...]
    dyT[:, tokens:] = dy_sib[...]
    step = 256
    for f in range(2):
        for p in range(nd):
            d = idx[1 + p]
            piece = pieces[p].at[pl.ds(f * size, size)]
            at = pl.multiple_of(d * rows, 8)
            wg[pl.ds(at, rows), :] = piece[0:rows]
            wu[pl.ds(at, rows), :] = piece[rows : 2 * rows]
            at = pl.multiple_of(d * quarter, 16)
            wd[pl.ds(at, quarter), 0:width] = piece[2 * rows : tail]
            wd[pl.ds(at, half), width:] = piece[tail:size, 0:rest]
            at = pl.multiple_of(d * quarter + half, 8)
            wd[pl.ds(at, half), width:] = piece[tail:size, rest:]
        wgT[...] = wg[...].T
        wuT[...] = wu[...].T
        wdT[...] = wd[...].T

        def opening(at):
            n, dy = nT[:, at : at + step], dyT[:, at : at + step]
            return dot(wgT[...], n), dot(wuT[...], n), dot(wd[...], dy)

        following = opening(0)
        for at in range(0, 2 * tokens, step):
            g, u, ga = following
            if at + step < 2 * tokens:
                following = opening(at + step)
            s = jax.nn.sigmoid(g)
            gs = g * s
            act = (gs * u).astype(BF16)
            du = (ga * gs).astype(BF16)
            dg = (ga * u * (s + gs * (1.0 - s))).astype(BF16)
            actT[:, at : at + step] = act
            dg_s[:, at : at + step] = dg
            du_s[:, at : at + step] = du
            out = dot(wdT[...], act)
            gn = dot(wg[...], dg) + dot(wu[...], du)
            r, to = at // tokens, at % tokens
            if f:
                out = out + sums[r][:, to : to + step].astype(F32)
                gn = gn + sums[2 + r][:, to : to + step].astype(F32)
            sums[r][:, to : to + step] = out.astype(BF16)
            sums[2 + r][:, to : to + step] = gn.astype(BF16)
        wg[...] = dot_nt(nT[...], dg_s[...]).astype(BF16)
        wu[...] = dot_nt(nT[...], du_s[...]).astype(BF16)
        wd[...] = dot_nt(actT[...], dyT[...]).astype(BF16)
        for p in range(nd):
            d = idx[1 + p]
            grads = stacks[p // (nd // 2)].at[pl.ds((p % (nd // 2) * 2 + f) * size, size)]
            at = pl.multiple_of(d * rows, 8)
            grads[0:rows] = wg[pl.ds(at, rows), :]
            grads[rows : 2 * rows] = wu[pl.ds(at, rows), :]
            at = pl.multiple_of(d * quarter, 16)
            grads[2 * rows : tail] = wd[pl.ds(at, quarter), 0:width]
            grads[tail:, 0:rest] = wd[pl.ds(at, half), width:]
            at = pl.multiple_of(d * quarter + half, 8)
            grads[tail:, rest:] = wd[pl.ds(at, half), width:]


def norm_backward(x, gain, grad):
    factor = lax.rsqrt(jnp.mean(x * x, axis=0, keepdims=True) + EPS)
    scaled = grad * gain
    along = jnp.mean(scaled * x, axis=0, keepdims=True)
    grad_x = factor * scaled - x * (factor * factor * factor * along)
    grad_gain = jnp.sum(grad * x * factor, axis=1, keepdims=True)
    return grad_x, grad_gain


def turn_kernel(
    idx, mid_ref, gain_ref, gn_own, gn_got, dy_ref, oT, lse, w_ref, *refs
):
    gmid_ref, half_ref, doT, stats, column = refs
    stats[0:16, :] = lse[...]
    delta = stats.at[16:32]
    mid = mid_ref[...]
    grad = gn_own[...].astype(F32) + gn_got[...].astype(F32)
    grad_mid, grad_gain = norm_backward(mid, gain_column(gain_ref, 1), grad)
    grad_mid = grad_mid + dy_ref[...].astype(F32)
    gmid_ref[...] = grad_mid
    half = grad_mid.astype(BF16)
    half_ref[...] = half
    heads = dot(w_ref[...], half).astype(BF16)
    doT[...] = heads
    for hd in range(QUERY_HEADS):
        rows = slice(hd * HEAD_SIZE, (hd + 1) * HEAD_SIZE)
        delta[hd : hd + 1, :] = jnp.sum(
            oT[rows, :].astype(F32) * heads[rows].astype(F32), axis=0, keepdims=True
        )
    delta[QUERY_HEADS:, :] = jnp.zeros_like(delta[QUERY_HEADS:, :])
    column[...] = jnp.broadcast_to(grad_gain, column.shape).astype(BF16)


def unrotate(head, cos, sin):
    half = HEAD_SIZE // 2
    g1, g2 = head[:half], head[half:]
    return jnp.concatenate([g1 * cos + g2 * sin, g2 * cos - g1 * sin], axis=0)


def query_kernel(nd, idx, dq, dq_got, cos, sin, nT, oT, half_ref, column, gq_ref, *parts):
    c, s = cos[...], sin[...]
    for hd in range(QUERY_HEADS):
        rows = slice(hd * HEAD_SIZE, (hd + 1) * HEAD_SIZE)
        gq_ref[rows, :] = unrotate(
            (dq[rows, :] + dq_got[rows, :].astype(F32)) * HEAD_SIZE**-0.5, c, s
        ).astype(BF16)
    model = half_ref.shape[0]
    rows = nT.shape[0] // nd
    offset, take = row_split(rows)
    for k in range(2):
        parity = idx[0] if k == 0 else 1 - idx[0]
        for p in range(nd):
            at = pl.ds(start_row(idx, 1 + k * nd + p, parity, rows, offset), take)
            part = parts[k].at[p * take : (p + 1) * take]
            part[:, 0:model] = dot_nt(oT[at, :], half_ref[...]).astype(BF16)
            part[:, model : model + 128] = column[at, :]
            part[:, model + 128 : 2 * model + 128] = dot_nt(nT[at, :], gq_ref[...]).astype(BF16)


def last_kernel(nd, terms, idx, x_ref, gain_ref, cos, sin, nT, gq, w_ref, gmid_ref, *refs):
    dkvs, refs = refs[:terms], refs[terms:]
    gx_ref, parts, gp, column = refs[0], refs[1:3], refs[3], refs[4]
    gkv = gp.at[QW : QW + 2 * KW]
    gp[0:QW] = gq[...]
    gp[QW + 2 * KW :] = jnp.zeros((gp.shape[0] - QW - 2 * KW, gp.shape[1]), BF16)
    c, s = cos[...], sin[...]
    for h in range(2 * KEY_VALUE_HEADS):
        rows = slice(h * HEAD_SIZE, (h + 1) * HEAD_SIZE)
        block = functools.reduce(lambda a, b: a + b, [t[rows, :].astype(F32) for t in dkvs])
        if h < KEY_VALUE_HEADS:
            block = unrotate(block, c, s)
        gkv[rows, :] = block.astype(BF16)
    wide = dot(w_ref[...], gp[...])
    x = x_ref[...].astype(F32)
    grad_x, grad_gain = norm_backward(x, gain_column(gain_ref, 0), wide)
    gx_ref[...] = (grad_x + gmid_ref[...]).astype(BF16)
    column[...] = jnp.broadcast_to(grad_gain, column.shape).astype(BF16)
    rows = nT.shape[0] // nd
    offset, take = row_split(rows)
    for k in range(2):
        parity = idx[0] if k == 0 else 1 - idx[0]
        for p in range(nd):
            at = pl.ds(start_row(idx, 1 + k * nd + p, parity, rows, offset), take)
            part = parts[k].at[p * take : (p + 1) * take]
            part[:, 0 : 2 * KW] = dot_nt(nT[at, :], gkv[...]).astype(BF16)
            part[:, 2 * KW :] = column[at, :]


def unpack_kernel(nd, pack_0, pack_1, gate, up, down_t):
    rows = gate.shape[0]
    quarter = down_t.shape[1] // 4
    width = nd * quarter
    half, rest, tail = quarter // 2, down_t.shape[0] - width, 2 * rows + quarter
    size = tail + half
    for core, packs in enumerate((pack_0, pack_1)):
        for f in range(2):
            pack = packs[f * size : (f + 1) * size].astype(F32)
            at = core * 2 * quarter + f * quarter
            for j in range(nd):
                dst = slice(j * 4 * quarter + at, j * 4 * quarter + at + quarter)
                src = slice(j * quarter, (j + 1) * quarter)
                gate[:, dst] = pack[0:rows, src]
                up[:, dst] = pack[rows : 2 * rows, src]
            last = jnp.concatenate([pack[tail:, 0:rest], pack[tail:, rest:]], axis=0)
            block = jnp.concatenate([pack[2 * rows : tail], last], axis=1)
            down_t[:, at : at + quarter] = block.T


def local(
    nd, nc, tokens, positions, w_qkv, w_out, w_gate, w_up, w_down, g_attn, g_mlp, grad_out
):
    plan = Plan(nd, nc)
    idx = plan.owners()
    x = tokens[0].T
    dy = grad_out[0].T
    model, count = x.shape
    shard = w_qkv.shape[0]
    offset, take = row_split(shard)
    start = plan.core * offset
    run = count // 2
    width = QW + 2 * KW

    def slice_rows(a):
        return lax.dynamic_slice_in_dim(a, start, take, 0)

    pad = jnp.zeros((take, 62), BF16)
    qkv_part = jnp.concatenate(
        [slice_rows(w_qkv), slice_rows(g_attn)[:, None], slice_rows(g_mlp)[:, None], pad], axis=1
    )
    dy_sib = plan.swap(dy)
    qkv_task = Task(plan.spread(qkv_part, plan.kd, plan.hop_d)).go(2)
    size = 2 * shard + w_down.shape[0] * 3 // 8
    mlp_width = w_gate.shape[1] // 4
    (pack,) = call(
        functools.partial(pack_kernel, nd),
        "pack",
        [((2 * size + shard * 3 // 2, mlp_width), BF16)],
        [idx, w_gate, w_up, w_down.T, w_out],
        smem=1,
        limit=12,
        us=4,
    )
    plan.gates = (pack,)
    qkv_parts = qkv_task.finish()
    plan.gates = ()
    qkv_sib = [plan.swap(p) for p in qkv_parts[:-1]]
    qkv_parts[-1] = after(qkv_parts[-1], dy_sib, *qkv_sib)
    qkv_sib.append(plan.swap(qkv_parts[-1]))
    plan.gates = qkv_parts[1:]
    pack_task = Task(plan.spread(pack, plan.kd, plan.hop_d)).go(2)

    pos = positions[0]
    q_blocks = pos[::run] // run
    half = HEAD_SIZE // 2
    freqs = THETA ** (-(jnp.arange(half).astype(F32) * 2.0) / HEAD_SIZE)
    angles = freqs[:, None] * pos.astype(F32)[None, :]
    cos, sin = jnp.cos(angles), jnp.sin(angles)

    normed, qT, kv, w_full, gains = call(
        functools.partial(project_kernel, nd),
        "project",
        [
            ((model, count), BF16),
            ((QW, count), BF16),
            ((2 * KW + 16, count), BF16),
            ((model, width + 64), BF16),
            ((model, 128), BF16),
        ],
        [after(idx, pack, dy_sib), pos[None], cos, sin, x] + qkv_parts + qkv_sib,
        smem=1,
        limit=20,
        us=6,
    )

    pieces = 1 << plan.kz
    plan.gates = (gains,)
    kv_sib = {0: plan.swap(kv)}
    kv_own = {0: kv}
    for j in range(plan.kz):
        kv_own[1 << j] = plan.hop_z(kv, j)
    qs = [qT, plan.swap(qT)]
    all_blocks = jnp.concatenate([q_blocks, kv_sib[0][2 * KW, ::run].astype(jnp.int32)])
    state = forward_wave(q_blocks, qT, [kv, kv_sib[0]], None, False, 8)
    for w in range(1, pieces):
        if w == 1:
            *state, kv_own[1], kv_own[2] = settle((*state, kv_own[1], kv_own[2]), pack_task)
        plan.gates = (state[0],)
        if w == 1:
            pack_task.go()
        for j in range(w.bit_length(), plan.kz):
            if w + (1 << j) not in kv_own:
                kv_own[w + (1 << j)] = plan.hop_z(kv_own[w], j)
        if w not in kv_sib:
            kv_sib[w] = plan.swap(kv_own[w])
        blocks = q_blocks
        if w == 1 and pieces > 2:
            kv_sib[2] = plan.swap(kv_own[2])
            blocks = after(blocks, kv_sib[2])
        state = forward_wave(blocks, qT, [kv_own[w], kv_sib[w]], state, w == pieces - 1, 8)
    pack_parts = pack_task.finish()
    oT, lse = settle(state, pack_task)

    plan.gates = (lse,)
    mid, normed_two, w_out_full = call(
        functools.partial(middle_kernel, nd),
        "middle",
        [((model, count), F32), ((model, count), BF16), ((QW, model), BF16)],
        [idx, x, oT, gains] + pack_parts,
        smem=1,
        limit=24,
        us=5,
    )
    normed_two_sib = plan.swap(normed_two)
    tall = nd * size
    got = call(
        functools.partial(mlp_kernel, nd),
        "mlp",
        [((model, count), BF16)] * 4 + [((tall, mlp_width), BF16)] * 2,
        [idx, normed_two, normed_two_sib, dy, dy_sib] + pack_parts,
        smem=1,
        scratch=[
            pltpu.VMEM((model, mlp_width), BF16),
            pltpu.VMEM((model, mlp_width), BF16),
            pltpu.VMEM((mlp_width, model), BF16),
            pltpu.VMEM((mlp_width, model), BF16),
            pltpu.VMEM((mlp_width, model), BF16),
            pltpu.VMEM((model, mlp_width), BF16),
            pltpu.VMEM((model, 2 * count), BF16),
            pltpu.VMEM((model, 2 * count), BF16),
            pltpu.VMEM((mlp_width, 2 * count), BF16),
            pltpu.VMEM((mlp_width, 2 * count), BF16),
            pltpu.VMEM((mlp_width, 2 * count), BF16),
        ],
        limit=44,
        us=36,
    )
    sums, (near, far) = got[:4], got[4:]
    plan.gates = ()
    gn_got = plan.swap(sums[3])
    pack_total = Task(plan.reduce_all(near, far)).go(1)
    turned = call(
        turn_kernel,
        "turn",
        [
            ((model, count), F32),
            ((model, count), BF16),
            ((QW, count), BF16),
            ((32, count), F32),
            ((model, 128), BF16),
        ],
        [idx, mid, gains, sums[2], gn_got, dy, oT, lse, w_out_full],
        smem=1,
        limit=30,
        us=8,
    )
    grad_mid, grad_half, doT, stats, column = turned
    plan.gates = (stats,)
    dos = [doT, plan.swap(doT)]
    both_stats = [stats, plan.swap(stats)]

    dq = None
    totals = {p: [] for p in range(pieces)}
    moved = []
    top = pieces - 1
    waits = {top - 1: (pack_total,), top - 2: (pack_total,)}
    for p in reversed(range(pieces)):
        got = backward_wave(
            all_blocks, qs, dos, both_stats, kv_own[p], totals[p] if p else [], dq, p == 0, 10
        )
        arrived = moved[-1:]
        got = settle(got, *waits.get(p, ()), *arrived)
        dkv = got[-1]
        plan.gates = (dkv,)
        if p:
            dq = got[0]
            j = p.bit_length() - 1
            moved.append(plan.hop_z(dkv, j))
            totals[p - (1 << j)].append(moved[-1])
        else:
            totals[0].append(dkv)
        if p in (top - 1, top - 2):
            pack_total.go(1)
    dq_got = plan.swap(got[1])
    wide = -(-(2 * model + 128) // 128) * 128
    stacked = ((nd * take, wide), BF16)
    gq, *parts = call(
        functools.partial(query_kernel, nd),
        "query",
        [((QW, count), BF16), stacked, stacked],
        [idx, got[0], dq_got, cos, sin, normed, oT, grad_half, column],
        smem=1,
        limit=22,
        us=4,
    )
    plan.gates = (gq,)

    def both_cores(own, stacked):
        other = plan.swap(stacked)
        half = own.shape[0] // 2
        return add(own[:half], other[:half]), add(own[half:], other[half:])

    gq, *parts = settle((gq, *parts), pack_total)
    near, far = both_cores(*parts)
    query_total = Task(plan.reduce_all(near, far, small=True)).go(1)
    pack_total.go(1)
    last_idx = after(idx, far)
    terms = totals[0]
    stacked = ((nd * take, 2 * KW + 128), BF16)
    grad_tokens, *parts = call(
        functools.partial(last_kernel, nd, len(terms)),
        "last",
        [((model, count), BF16), stacked, stacked],
        [last_idx, x, gains, cos, sin, normed, gq, w_full, grad_mid] + terms,
        smem=1,
        scratch=[pltpu.VMEM((width + 64, count), BF16), pltpu.VMEM((model, 128), BF16)],
        limit=28,
        us=6,
    )
    plan.gates = (parts[0],)
    out_got = plan.swap(sums[1])
    output = (mid + (sums[0].astype(F32) + out_got.astype(F32))).astype(BF16)
    kv_total = Task(plan.reduce_all(*both_cores(*parts), small=True))
    kv_halves = kv_total.finish()
    query_halves = query_total.finish()
    gate, up, down = call(
        functools.partial(unpack_kernel, nd),
        "unpack",
        [(w.shape, F32) for w in (w_gate, w_up, w_down.T)],
        list(pack_total.finish()),
        limit=24,
        us=6,
    )

    def whole(halves):
        low, high = halves
        return jnp.concatenate([low, high[2 * take - shard :]], axis=0).astype(F32)

    query_whole = whole(query_halves)
    kv_whole = whole(kv_halves)
    qkv_whole = jnp.concatenate(
        [query_whole[:, model + 128 : 2 * model + 128], kv_whole[:, : 2 * KW]], axis=1
    )
    return (
        output.T[None],
        grad_tokens.T[None],
        qkv_whole,
        query_whole[:, :model],
        gate,
        up,
        down.T,
        kv_whole[:, 2 * KW],
        query_whole[:, model],
    )


def solution(mesh):
    rows = P("dp", None)
    stored = P("dp", "ctx", None)
    vector = P("dp")
    return jax.shard_map(
        functools.partial(local, mesh.shape["dp"], mesh.shape["ctx"]),
        mesh=mesh,
        in_specs=(stored, P("dp", "ctx"), rows, rows, rows, rows, rows, vector, vector, stored),
        out_specs=(stored, stored, rows, rows, rows, rows, rows, vector, vector),
        check_vma=False,
    )
```

profile of v0, /device:TPU:0, one launch (start us, length us, event | category | flops | bytes accessed | tf_op | source)
XLA Modules:
  0.0 370.0 jit_solution(17853436199871373296)
XLA Ops:
  2.4 2.7 collective-permute-start.1
  14.7 2.8 collective-permute-start.3
  17.9 5.8 %collective-permute-done.3.refs_3_ = bf16[128,1664]{1,0:T(8,128)(2,1)S(1)} collective-permute-done((bf16[128,1664]{1,0:T(8,128)(2,1)}, bf16[128,1664]{1,0:T(8,128)(2,1)S(1)}, u32[]{:S(2)}, u32[]{:S(2)}) %collective-permute-start.3) | collective-permute-done | bytes 426016 | tf_op jit(solution)/shard_map/ppermute | solution.py:88
  23.7 1.9 collective-permute-start.11
  25.7 1.8 collective-permute-start.12
  30.2 5.2 %project.1 = (bf16[960,512]{1,0:T(8,128)(2,1)S(1)}, bf16[960,512]{1,0:T(8,128)(2,1)S(1)}, bf16[656,512]{1,0:T(8,128)(2,1)}, bf16[960,1664]{1,0:T(8,128)(2,1)S(1)}, bf16[960,128]{1,0:T(8,128)(2,1)S(1)}) custom-call(s32[9]{0:T(128)S(1)} %pad_add_fusion.idx, s32[1,512]{1,0:T(1,128)S(1)} %copy-done.45, f32[32,512]{1,0:T(8,128)S(1)} %get-tuple-element.242.cos, ...), custom_call_target="tpu_custom_call" | custom-call | flops 60000000 | tf_op jit(solution)/shard_map/project/pallas_call | solution.py:38
  38.2 2.6 collective-permute-start.10
  42.5 8.7 %attention_forward.4 = (f32[16,512]{1,0:T(8,128)S(1)}, f32[16,512]{1,0:T(8,128)S(1)}, f32[960,512]{1,0:T(8,128)S(1)}) custom-call(s32[2]{0:T(128)S(1)} %and_select_fusion.q_blocks, bf16[960,512]{1,0:T(8,128)(2,1)S(1)} %get-tuple-element.155.qT.refs_0_, bf16[656,512]{1,0:T(8,128)(2,1)} %get-tuple-element.125.refs_0_.refs_6_, ...), custom_call_target="tpu_custom_call" | custom-call | flops 80000000 | tf_op jit(solution)/shard_map/attention_forward/pallas_call | solution.py:38
  51.2 19.2 %collective-permute-done.10.refs_0_.refs_6_ = bf16[656,512]{1,0:T(8,128)(2,1)} collective-permute-done((bf16[656,512]{1,0:T(8,128)(2,1)}, bf16[656,512]{1,0:T(8,128)(2,1)}, u32[]{:S(2)}, u32[]{:S(2)}) %collective-permute-start.10) | collective-permute-done | bytes 671776 | tf_op jit(solution)/shard_map/ppermute | solution.py:98
  70.4 5.0 %collective-permute-done.11.refs_1_ = bf16[1800,640]{1,0:T(8,128)(2,1)} collective-permute-done((bf16[1800,640]{1,0:T(8,128)(2,1)S(1)}, bf16[1800,640]{1,0:T(8,128)(2,1)}, u32[]{:S(2)}, u32[]{:S(2)}) %collective-permute-start.11) | collective-permute-done | bytes 2304032 | tf_op jit(solution)/shard_map/ppermute | solution.py:88
  77.0 2.1 collective-permute-start.13
  79.8 7.7 %attention_forward.5 = (f32[16,512]{1,0:T(8,128)S(1)}, f32[16,512]{1,0:T(8,128)S(1)}, f32[960,512]{1,0:T(8,128)S(1)}) custom-call(s32[2]{0:T(128)S(1)} %and_select_fusion.q_blocks, bf16[960,512]{1,0:T(8,128)(2,1)S(1)} %get-tuple-element.155.qT.refs_0_, bf16[656,512]{1,0:T(8,128)(2,1)} %collective-permute-done.9.refs_0_.refs_6_, ...), custom_call_target="tpu_custom_call" | custom-call | flops 80000000 | tf_op jit(solution)/shard_map/attention_forward/pallas_call | solution.py:38
  87.4 7.9 %attention_forward.6 = (f32[16,512]{1,0:T(8,128)S(1)}, f32[16,512]{1,0:T(8,128)S(1)}, f32[960,512]{1,0:T(8,128)S(1)}) custom-call(s32[2]{0:T(128)S(1)} %and_select_fusion.q_blocks, bf16[960,512]{1,0:T(8,128)(2,1)S(1)} %get-tuple-element.155.qT.refs_0_, bf16[656,512]{1,0:T(8,128)(2,1)} %collective-permute-done.10.refs_0_.refs_6_, ...), custom_call_target="tpu_custom_call" | custom-call | flops 80000000 | tf_op jit(solution)/shard_map/attention_forward/pallas_call | solution.py:38
  96.0 2.1 collective-permute-done.16.refs_1_
  98.2 7.2 %attention_forward.7 = (bf16[960,512]{1,0:T(8,128)(2,1)S(1)}, f32[16,512]{1,0:T(8,128)S(1)}) custom-call(s32[2]{0:T(128)S(1)} %and_select_fusion.q_blocks, bf16[960,512]{1,0:T(8,128)(2,1)S(1)} %get-tuple-element.155.qT.refs_0_, bf16[656,512]{1,0:T(8,128)(2,1)S(1)} %collective-permute-done.13.refs_0_.refs_6_, ...), custom_call_target="tpu_custom_call" | custom-call | flops 80000000 | tf_op jit(solution)/shard_map/attention_forward/pallas_call | solution.py:38
  105.4 5.6 %middle.1 = (f32[960,512]{1,0:T(8,128)S(1)}, bf16[960,512]{1,0:T(8,128)(2,1)S(1)}, bf16[960,960]{1,0:T(8,128)(2,1)S(1)}) custom-call(s32[9]{0:T(128)S(1)} %pad_add_fusion.idx, bf16[960,512]{1,0:T(8,128)(2,1)S(1)} %bitcast.26, bf16[960,512]{1,0:T(8,128)(2,1)S(1)} %get-tuple-element.148.oT, bf16[960,128]{1,0:T(8,128)(2,1)S(1)} %get-tuple-element.124.gain_ref, ...), custom_call_target="tpu_custom_call" | custom-call | flops 50000000 | tf_op jit(solution)/shard_map/middle/pallas_call | solution.py:38
  111.3 2.4 collective-permute-done.18.n_sib
  113.7 43.2 %mlp.1 = (bf16[960,512]{1,0:T(8,128)(2,1)S(1)}, bf16[960,512]{1,0:T(8,128)(2,1)S(1)}, bf16[960,512]{1,0:T(8,128)(2,1)S(1)}, bf16[960,512]{1,0:T(8,128)(2,1)S(1)}...) custom-call(s32[9]{0:T(128)S(1)} %pad_add_fusion.idx, bf16[960,512]{1,0:T(8,128)(2,1)S(1)} %get-tuple-element.152.n_own, ...), custom_call_target="tpu_custom_call" | custom-call | flops 360000000 | tf_op jit(solution)/shard_map/mlp/pallas_call | solution.py:38
  159.5 2.2 collective-permute-done.20.gn_got
  161.7 3.0 turn.1
  171.4 9.8 %attention_backward.4 = (f32[2,960,512]{2,1,0:T(8,128)S(1)}, bf16[640,512]{1,0:T(8,128)(2,1)S(1)}) custom-call(s32[4]{0:T(128)S(1)} %pad_add_fusion.1.q_blocks, bf16[960,512]{1,0:T(8,128)(2,1)S(1)} %get-tuple-element.155.qT.refs_0_, bf16[960,512]{1,0:T(8,128)(2,1)S(1)} %collective-permute-done.19.refs_1_, bf16[960,512]{1,0:T(8,128)(2,1)S(1)} %get-tuple-element.161.refs_2_, ...), custom_call_target="tpu_custom_call" | custom-call | flops 100000000 | tf_op jit(solution)/shard_map/attention_backward/pallas_call | solution.py:38
  181.2 1.8 collective-permute-start.23
  183.0 11.0 %attention_backward.5 = (f32[2,960,512]{2,1,0:T(8,128)S(1)}, bf16[640,512]{1,0:T(8,128)(2,1)}) custom-call(s32[4]{0:T(128)S(1)} %pad_add_fusion.1.q_blocks, bf16[960,512]{1,0:T(8,128)(2,1)S(1)} %get-tuple-element.155.qT.refs_0_, bf16[960,512]{1,0:T(8,128)(2,1)S(1)} %collective-permute-done.19.refs_1_, bf16[960,512]{1,0:T(8,128)(2,1)S(1)} %get-tuple-element.161.refs_2_, ...), custom_call_target="tpu_custom_call" | custom-call | flops 100000000 | tf_op jit(solution)/shard_map/attention_backward/pallas_call | solution.py:38
  194.0 5.7 %collective-permute-done.23.refs_7_ = bf16[640,512]{1,0:T(8,128)(2,1)S(1)} collective-permute-done((bf16[640,512]{1,0:T(8,128)(2,1)S(1)}, bf16[640,512]{1,0:T(8,128)(2,1)S(1)}, u32[]{:S(2)}, u32[]{:S(2)}) %collective-permute-start.23) | collective-permute-done | bytes 655392 | tf_op jit(solution)/shard_map/ppermute | solution.py:98
  201.3 3.2 add_convert_fusion.1
  207.8 2.1 copy-done.11
  211.0 10.0 %attention_backward.6 = (f32[2,960,512]{2,1,0:T(8,128)S(1)}, bf16[640,512]{1,0:T(8,128)(2,1)S(1)}) custom-call(s32[4]{0:T(128)S(1)} %pad_add_fusion.1.q_blocks, bf16[960,512]{1,0:T(8,128)(2,1)S(1)} %get-tuple-element.155.qT.refs_0_, bf16[960,512]{1,0:T(8,128)(2,1)S(1)} %collective-permute-done.19.refs_1_, bf16[960,512]{1,0:T(8,128)(2,1)S(1)} %get-tuple-element.161.refs_2_, ...), custom_call_target="tpu_custom_call" | custom-call | flops 100000000 | tf_op jit(solution)/shard_map/attention_backward/pallas_call | solution.py:38
  220.9 4.1 %collective-permute-done.26.refs_0_ = bf16[640,512]{1,0:T(8,128)(2,1)} collective-permute-done((bf16[640,512]{1,0:T(8,128)(2,1)}, bf16[640,512]{1,0:T(8,128)(2,1)}, u32[]{:S(2)}, u32[]{:S(2)}) %collective-permute-start.26) | collective-permute-done | bytes 655392 | tf_op jit(solution)/shard_map/ppermute | solution.py:98
  225.0 3.1 collective-permute-done.25
  228.4 11.8 %attention_backward.7 = (f32[960,512]{1,0:T(8,128)S(1)}, bf16[960,512]{1,0:T(8,128)(2,1)S(1)}, bf16[640,512]{1,0:T(8,128)(2,1)S(1)}) custom-call(s32[4]{0:T(128)S(1)} %pad_add_fusion.1.q_blocks, bf16[960,512]{1,0:T(8,128)(2,1)S(1)} %get-tuple-element.155.qT.refs_0_, bf16[960,512]{1,0:T(8,128)(2,1)S(1)} %collective-permute-done.19.refs_1_, ...), custom_call_target="tpu_custom_call" | custom-call | flops 100000000 | tf_op jit(solution)/shard_map/attention_backward/pallas_call | solution.py:38
  240.3 3.0 add_convert_fusion
  243.3 1.8 collective-permute-done.27.refs_1_
  247.8 6.9 %query.1 = (bf16[960,512]{1,0:T(8,128)(2,1)S(1)}, bf16[512,2048]{1,0:T(8,128)(2,1)S(1)}, bf16[512,2048]{1,0:T(8,128)(2,1)}) custom-call(s32[9]{0:T(128)S(1)} %pad_add_fusion.idx, f32[960,512]{1,0:T(8,128)S(1)} %get-tuple-element.182.dq, bf16[960,512]{1,0:T(8,128)(2,1)S(1)} %collective-permute-done.28.dq_got, f32[32,512]{1,0:T(8,128)S(1)} %copy-done.29, ...), custom_call_target="tpu_custom_call" | custom-call | flops 40000000 | tf_op jit(solution)/shard_map/query/pallas_call | solution.py:38
  255.6 13.7 %collective-permute-done.29 = bf16[720,640]{1,0:T(8,128)(2,1)S(1)} collective-permute-done((bf16[720,640]{1,0:T(8,128)(2,1)S(1)}, bf16[720,640]{1,0:T(8,128)(2,1)S(1)}, u32[]{:S(2)}, u32[]{:S(2)}) %collective-permute-start.29) | collective-permute-done | bytes 921632 | tf_op jit(solution)/shard_map/ppermute | solution.py:98
  270.2 1.8 add_convert_fusion.5
  274.7 3.6 add_convert_fusion.2
  278.4 6.6 %last.1 = (bf16[960,512]{1,0:T(8,128)(2,1)}, bf16[512,768]{1,0:T(8,128)(2,1)S(1)}, bf16[512,768]{1,0:T(8,128)(2,1)}) custom-call(s32[9]{0:T(128)S(1)} %pad_add_fusion.idx, bf16[960,512]{1,0:T(8,128)(2,1)S(1)} %bitcast.27, bf16[960,128]{1,0:T(8,128)(2,1)S(1)} %get-tuple-element.124.gain_ref, f32[32,512]{1,0:T(8,128)S(1)} %copy-done.29, ...), custom_call_target="tpu_custom_call" | custom-call | flops 60000000 | tf_op jit(solution)/shard_map/last/pallas_call | solution.py:38
  288.1 10.1 %collective-permute-done.44 = bf16[360,640]{1,0:T(8,128)(2,1)S(1)} collective-permute-done((bf16[360,640]{1,0:T(8,128)(2,1)S(1)}, bf16[360,640]{1,0:T(8,128)(2,1)S(1)}, u32[]{:S(2)}, u32[]{:S(2)}) %collective-permute-start.44) | collective-permute-done | bytes 460832 | tf_op jit(solution)/shard_map/ppermute | solution.py:98
  298.4 2.0 collective-permute-start.45
  303.6 1.8 collective-permute-start.33
  305.4 6.6 %collective-permute-done.38 = bf16[256,768]{1,0:T(8,128)(2,1)S(1)} collective-permute-done((bf16[256,768]{1,0:T(8,128)(2,1)S(1)}, bf16[256,768]{1,0:T(8,128)(2,1)S(1)}, u32[]{:S(2)}, u32[]{:S(2)}) %collective-permute-start.38) | collective-permute-done | bytes 393248 | tf_op jit(solution)/shard_map/ppermute | solution.py:88
  312.0 2.3 collective-permute-start.39
  315.7 2.3 collective-permute-done.39
  318.1 2.8 collective-permute-start.40
  322.5 3.1 collective-permute-done.45
  326.8 15.9 %collective-permute-done.34 = bf16[128,2048]{1,0:T(8,128)(2,1)S(1)} collective-permute-done((bf16[128,2048]{1,0:T(8,128)(2,1)S(1)}, bf16[128,2048]{1,0:T(8,128)(2,1)S(1)}, u32[]{:S(2)}, u32[]{:S(2)}) %collective-permute-start.34) | collective-permute-done | bytes 524320 | tf_op jit(solution)/shard_map/ppermute | solution.py:98
  343.8 14.3 %collective-permute-done.35 = bf16[128,2048]{1,0:T(8,128)(2,1)S(1)} collective-permute-done((bf16[128,2048]{1,0:T(8,128)(2,1)S(1)}, bf16[128,2048]{1,0:T(8,128)(2,1)S(1)}, u32[]{:S(2)}, u32[]{:S(2)}) %collective-permute-start.35) | collective-permute-done | bytes 524320 | tf_op jit(solution)/shard_map/ppermute | solution.py:98
  364.7 5.0 %unpack.1 = (f32[240,2560]{1,0:T(8,128)}, f32[240,2560]{1,0:T(8,128)}, f32[960,640]{1,0:T(8,128)}) custom-call(bf16[1440,640]{1,0:T(8,128)(2,1)S(1)} %get-tuple-element.232.pack_0, bf16[1440,640]{1,0:T(8,128)(2,1)S(1)} %get-tuple-element.231.pack_1), custom_call_target="tpu_custom_call" | custom-call | flops 60000000 | tf_op jit(solution)/shard_map/unpack/pallas_call | solution.py:38
  (220 shorter events, 63.0 us)
Async XLA Ops:
  0.7 23.1 %collective-permute-start = (bf16[960,512]{1,0:T(8,128)(2,1)}, bf16[960,512]{1,0:T(8,128)(2,1)}, u32[]{:S(2)}, u32[]{:S(2)}) collective-permute-start(bf16[960,512]{1,0:T(8,128)(2,1)} %bitcast.28), channel_id=1, source_target_pairs={{0,1},{1,0},{2,3},{3,2},{4,5},{5,4},{6,7},{7,6},{8,9},{9,8},{10,11... | collective-permute-start | bytes 2949128 | tf_op jit(solution)/shard_map/ppermute | solution.py:102
  2.4 12.2 %collective-permute-start.1 = (bf16[128,1664]{1,0:T(8,128)(2,1)S(1)}, bf16[128,1664]{1,0:T(8,128)(2,1)}, u32[]{:S(2)}, u32[]{:S(2)}) collective-permute-start(bf16[128,1664]{1,0:T(8,128)(2,1)S(1)} %concatenate.25.refs_0_), channel_id=1, source_target_pairs={{0,8},{1,17},{2,10},{3,19},{4,12},{5,21},{6,14},{7,23},{8,0},{9,25... | collective-permute-start | bytes 1277960 | tf_op jit(solution)/shard_map/ppermute | solution.py:88
  5.1 12.3 %collective-permute-start.2 = (bf16[128,1664]{1,0:T(8,128)(2,1)S(1)}, bf16[128,1664]{1,0:T(8,128)(2,1)}, u32[]{:S(2)}, u32[]{:S(2)}) collective-permute-start(bf16[128,1664]{1,0:T(8,128)(2,1)S(1)} %concatenate.25.refs_0_), channel_id=1, source_target_pairs={{0,16},{1,9},{2,18},{3,11},{4,20},{5,13},{6,22},{7,15},{8,24},{9,1... | collective-permute-start | bytes 1277960 | tf_op jit(solution)/shard_map/ppermute | solution.py:88
  6.6 11.3 %collective-permute-start.4 = (bf16[128,1664]{1,0:T(8,128)(2,1)S(1)}, bf16[128,1664]{1,0:T(8,128)(2,1)}, u32[]{:S(2)}, u32[]{:S(2)}) collective-permute-start(bf16[128,1664]{1,0:T(8,128)(2,1)S(1)} %concatenate.25.refs_0_), channel_id=1, source_target_pairs={{0,1},{1,0},{2,3},{3,2},{4,5},{5,4},{6,7},{7,6},{8,9},{9,8},{10,11... | collective-permute-start | bytes 1277960 | tf_op jit(solution)/shard_map/ppermute | solution.py:102
  14.7 9.1 %collective-permute-start.3 = (bf16[128,1664]{1,0:T(8,128)(2,1)}, bf16[128,1664]{1,0:T(8,128)(2,1)S(1)}, u32[]{:S(2)}, u32[]{:S(2)}) collective-permute-start(bf16[128,1664]{1,0:T(8,128)(2,1)} %collective-permute-done.1.refs_1_), channel_id=1, source_target_pairs={{0,16},{1,9},{2,18},{3,11},{4,20},{5,13},{6,22},{7,15},{8,24},{9,1... | collective-permute-start | bytes 1277960 | tf_op jit(solution)/shard_map/ppermute | solution.py:88
  17.4 6.3 %collective-permute-start.5 = (bf16[128,1664]{1,0:T(8,128)(2,1)}, bf16[128,1664]{1,0:T(8,128)(2,1)S(1)}, u32[]{:S(2)}, u32[]{:S(2)}) collective-permute-start(bf16[128,1664]{1,0:T(8,128)(2,1)} %collective-permute-done.1.refs_1_), channel_id=1, source_target_pairs={{0,1},{1,0},{2,3},{3,2},{4,5},{5,4},{6,7},{7,6},{8,9},{9,8},{10,11... | collective-permute-start | bytes 1277960 | tf_op jit(solution)/shard_map/ppermute | solution.py:102
  17.4 6.3 %collective-permute-start.6 = (bf16[128,1664]{1,0:T(8,128)(2,1)}, bf16[128,1664]{1,0:T(8,128)(2,1)S(1)}, u32[]{:S(2)}, u32[]{:S(2)}) collective-permute-start(bf16[128,1664]{1,0:T(8,128)(2,1)} %collective-permute-done.2.refs_2_), channel_id=1, source_target_pairs={{0,1},{1,0},{2,3},{3,2},{4,5},{5,4},{6,7},{7,6},{8,9},{9,8},{10,11... | collective-permute-start | bytes 1277960 | tf_op jit(solution)/shard_map/ppermute | solution.py:102
  23.7 51.7 %collective-permute-start.11 = (bf16[1800,640]{1,0:T(8,128)(2,1)S(1)}, bf16[1800,640]{1,0:T(8,128)(2,1)}, u32[]{:S(2)}, u32[]{:S(2)}) collective-permute-start(bf16[1800,640]{1,0:T(8,128)(2,1)S(1)} %pack.1.refs_0_), channel_id=1, source_target_pairs={{0,8},{1,17},{2,10},{3,19},{4,12},{5,21},{6,14},{7,23},{8,0},{9,25... | collective-permute-start | bytes 6912008 | tf_op jit(solution)/shard_map/ppermute | solution.py:88
  25.7 49.8 %collective-permute-start.12 = (bf16[1800,640]{1,0:T(8,128)(2,1)S(1)}, bf16[1800,640]{1,0:T(8,128)(2,1)}, u32[]{:S(2)}, u32[]{:S(2)}) collective-permute-start(bf16[1800,640]{1,0:T(8,128)(2,1)S(1)} %pack.1.refs_0_), channel_id=1, source_target_pairs={{0,16},{1,9},{2,18},{3,11},{4,20},{5,13},{6,22},{7,15},{8,24},{9,1... | collective-permute-start | bytes 6912008 | tf_op jit(solution)/shard_map/ppermute | solution.py:88
  27.5 1.8 collective-permute-start.7
  38.1 4.4 %collective-permute-start.8 = (bf16[656,512]{1,0:T(8,128)(2,1)}, bf16[656,512]{1,0:T(8,128)(2,1)}, u32[]{:S(2)}, u32[]{:S(2)}) collective-permute-start(bf16[656,512]{1,0:T(8,128)(2,1)} %get-tuple-element.125.refs_0_.refs_6_), channel_id=1, source_target_pairs={{0,1},{1,0},{2,3},{3,2},{4,5},{5,4},{6,7},{7,6},{8,9},{9,8},{10,11... | collective-permute-start | bytes 2015240 | tf_op jit(solution)/shard_map/ppermute | solution.py:102
  38.2 32.2 %collective-permute-start.10 = (bf16[656,512]{1,0:T(8,128)(2,1)}, bf16[656,512]{1,0:T(8,128)(2,1)}, u32[]{:S(2)}, u32[]{:S(2)}) collective-permute-start(bf16[656,512]{1,0:T(8,128)(2,1)} %get-tuple-element.125.refs_0_.refs_6_), channel_id=1, source_target_pairs={{0,4},{1,3},{2,6},{3,1},{4,0},{5,7},{6,2},{7,5},{8,12},{9,11},{10,... | collective-permute-start | bytes 2015240 | tf_op jit(solution)/shard_map/ppermute | solution.py:98
  40.8 29.6 %collective-permute-start.9 = (bf16[656,512]{1,0:T(8,128)(2,1)}, bf16[656,512]{1,0:T(8,128)(2,1)}, u32[]{:S(2)}, u32[]{:S(2)}) collective-permute-start(bf16[656,512]{1,0:T(8,128)(2,1)} %get-tuple-element.125.refs_0_.refs_6_), channel_id=1, source_target_pairs={{0,2},{1,5},{2,0},{3,7},{4,6},{5,1},{6,4},{7,3},{8,10},{9,13},{10,... | collective-permute-start | bytes 2015240 | tf_op jit(solution)/shard_map/ppermute | solution.py:98
  75.4 29.9 %collective-permute-start.17 = (bf16[1800,640]{1,0:T(8,128)(2,1)}, bf16[1800,640]{1,0:T(8,128)(2,1)S(1)}, u32[]{:S(2)}, u32[]{:S(2)}) collective-permute-start(bf16[1800,640]{1,0:T(8,128)(2,1)} %collective-permute-done.11.refs_1_), channel_id=1, source_target_pairs={{0,16},{1,9},{2,18},{3,11},{4,20},{5,13},{6,22},{7,15},{8,24},{9,1... | collective-permute-start | bytes 6912008 | tf_op jit(solution)/shard_map/ppermute | solution.py:88
  76.5 2.6 collective-permute-start.14
  76.5 3.3 collective-permute-start.15
  77.0 19.1 %collective-permute-start.13 = (bf16[656,512]{1,0:T(8,128)(2,1)}, bf16[656,512]{1,0:T(8,128)(2,1)S(1)}, u32[]{:S(2)}, u32[]{:S(2)}) collective-permute-start(bf16[656,512]{1,0:T(8,128)(2,1)} %collective-permute-done.9.refs_0_.refs_6_), channel_id=1, source_target_pairs={{0,4},{1,3},{2,6},{3,1},{4,0},{5,7},{6,2},{7,5},{8,12},{9,11},{10,... | collective-permute-start | bytes 2015240 | tf_op jit(solution)/shard_map/ppermute | solution.py:98
  96.0 2.1 collective-permute-start.16
  105.4 56.3 %copy-start.3 = (bf16[960,512]{1,0:T(8,128)(2,1)}, bf16[960,512]{1,0:T(8,128)(2,1)S(1)}, u32[]{:S(2)}) copy-start(bf16[960,512]{1,0:T(8,128)(2,1)S(1)} %get-tuple-element.148.oT) | copy-start | bytes 2949124
  111.1 2.6 collective-permute-start.18
  157.9 43.4 %collective-permute-start.24 = (bf16[2880,640]{1,0:T(8,128)(2,1)}, bf16[2880,640]{1,0:T(8,128)(2,1)}, u32[]{:S(2)}, u32[]{:S(2)}) collective-permute-start(bf16[2880,640]{1,0:T(8,128)(2,1)} %get-tuple-element.167), channel_id=1, source_target_pairs={{0,16},{1,9},{2,18},{3,11},{4,20},{5,13},{6,22},{7,15},{8,24},{9,1... | collective-permute-start | bytes 11059208 | tf_op jit(solution)/shard_map/ppermute | solution.py:88
  158.1 3.6 collective-permute-start.20
  159.5 9.5 %collective-permute-start.19 = (bf16[960,512]{1,0:T(8,128)(2,1)S(1)}, bf16[960,512]{1,0:T(8,128)(2,1)S(1)}, u32[]{:S(2)}, u32[]{:S(2)}) collective-permute-start(bf16[960,512]{1,0:T(8,128)(2,1)S(1)} %get-tuple-element.155.qT.refs_0_), channel_id=1, source_target_pairs={{0,1},{1,0},{2,3},{3,2},{4,5},{5,4},{6,7},{7,6},{8,9},{9,8},{10,11... | collective-permute-start | bytes 2949128 | tf_op jit(solution)/shard_map/ppermute | solution.py:102
  167.6 2.7 collective-permute-start.21
  168.8 1.5 collective-permute-start.22
  181.2 18.6 %collective-permute-start.23 = (bf16[640,512]{1,0:T(8,128)(2,1)S(1)}, bf16[640,512]{1,0:T(8,128)(2,1)S(1)}, u32[]{:S(2)}, u32[]{:S(2)}) collective-permute-start(bf16[640,512]{1,0:T(8,128)(2,1)S(1)} %get-tuple-element.163), channel_id=1, source_target_pairs={{0,4},{1,3},{2,6},{3,1},{4,0},{5,7},{6,2},{7,5},{8,12},{9,11},{10,... | collective-permute-start | bytes 1966088 | tf_op jit(solution)/shard_map/ppermute | solution.py:98
  204.5 23.6 %collective-permute-start.25 = (bf16[1440,640]{1,0:T(8,128)(2,1)}, bf16[1440,640]{1,0:T(8,128)(2,1)}, u32[]{:S(2)}, u32[]{:S(2)}) collective-permute-start(bf16[1440,640]{1,0:T(8,128)(2,1)} %add_convert_fusion.1), channel_id=1, source_target_pairs={{0,8},{1,17},{2,10},{3,19},{4,12},{5,21},{6,14},{7,23},{8,0},{9,25... | collective-permute-start | bytes 5529608 | tf_op jit(solution)/shard_map/ppermute | solution.py:88
  206.2 18.8 %collective-permute-start.26 = (bf16[640,512]{1,0:T(8,128)(2,1)}, bf16[640,512]{1,0:T(8,128)(2,1)}, u32[]{:S(2)}, u32[]{:S(2)}) collective-permute-start(bf16[640,512]{1,0:T(8,128)(2,1)} %get-tuple-element.175), channel_id=1, source_target_pairs={{0,4},{1,3},{2,6},{3,1},{4,0},{5,7},{6,2},{7,5},{8,12},{9,11},{10,... | collective-permute-start | bytes 1966088 | tf_op jit(solution)/shard_map/ppermute | solution.py:98
  228.1 17.0 %collective-permute-start.27 = (bf16[640,512]{1,0:T(8,128)(2,1)S(1)}, bf16[640,512]{1,0:T(8,128)(2,1)S(1)}, u32[]{:S(2)}, u32[]{:S(2)}) collective-permute-start(bf16[640,512]{1,0:T(8,128)(2,1)S(1)} %get-tuple-element.181), channel_id=1, source_target_pairs={{0,2},{1,5},{2,0},{3,7},{4,6},{5,1},{6,4},{7,3},{8,10},{9,13},{10,... | collective-permute-start | bytes 1966088 | tf_op jit(solution)/shard_map/ppermute | solution.py:98
  245.2 2.6 collective-permute-start.28
  245.2 24.0 %collective-permute-start.29 = (bf16[720,640]{1,0:T(8,128)(2,1)S(1)}, bf16[720,640]{1,0:T(8,128)(2,1)S(1)}, u32[]{:S(2)}, u32[]{:S(2)}) collective-permute-start(bf16[720,640]{1,0:T(8,128)(2,1)S(1)} %constant_dynamic-slice_fusion.1), channel_id=1, source_target_pairs={{0,4},{1,3},{2,6},{3,1},{4,0},{5,7},{6,2},{7,5},{8,12},{9,11},{10,... | collective-permute-start | bytes 2764808 | tf_op jit(solution)/shard_map/ppermute | solution.py:98
  270.2 4.5 %collective-permute-start.30 = (bf16[512,2048]{1,0:T(8,128)(2,1)}, bf16[512,2048]{1,0:T(8,128)(2,1)}, u32[]{:S(2)}, u32[]{:S(2)}) collective-permute-start(bf16[512,2048]{1,0:T(8,128)(2,1)} %get-tuple-element.196), channel_id=1, source_target_pairs={{0,1},{1,0},{2,3},{3,2},{4,5},{5,4},{6,7},{7,6},{8,9},{9,8},{10,11... | collective-permute-start | bytes 6291464 | tf_op jit(solution)/shard_map/ppermute | solution.py:102
  272.1 13.2 %collective-permute-start.43 = (bf16[360,640]{1,0:T(8,128)(2,1)S(1)}, bf16[360,640]{1,0:T(8,128)(2,1)S(1)}, u32[]{:S(2)}, u32[]{:S(2)}) collective-permute-start(bf16[360,640]{1,0:T(8,128)(2,1)S(1)} %constant_dynamic-slice_fusion), channel_id=1, source_target_pairs={{0,2},{1,5},{2,0},{3,7},{4,6},{5,1},{6,4},{7,3},{8,10},{9,13},{10,... | collective-permute-start | bytes 1382408 | tf_op jit(solution)/shard_map/ppermute | solution.py:98
  285.4 12.8 %collective-permute-start.44 = (bf16[360,640]{1,0:T(8,128)(2,1)S(1)}, bf16[360,640]{1,0:T(8,128)(2,1)S(1)}, u32[]{:S(2)}, u32[]{:S(2)}) collective-permute-start(bf16[360,640]{1,0:T(8,128)(2,1)S(1)} %add_convert_fusion.10), channel_id=1, source_target_pairs={{0,2},{1,5},{2,0},{3,7},{4,6},{5,1},{6,4},{7,3},{8,10},{9,13},{10,... | collective-permute-start | bytes 1382408 | tf_op jit(solution)/shard_map/ppermute | solution.py:98
  286.0 14.4 %collective-permute-start.37 = (bf16[512,768]{1,0:T(8,128)(2,1)}, bf16[512,768]{1,0:T(8,128)(2,1)S(1)}, u32[]{:S(2)}, u32[]{:S(2)}) collective-permute-start(bf16[512,768]{1,0:T(8,128)(2,1)} %get-tuple-element.212), channel_id=1, source_target_pairs={{0,1},{1,0},{2,3},{3,2},{4,5},{5,4},{6,7},{7,6},{8,9},{9,8},{10,11... | collective-permute-start | bytes 2359304 | tf_op jit(solution)/shard_map/ppermute | solution.py:102
  286.0 16.3 %collective-permute-start.32 = (bf16[256,2048]{1,0:T(8,128)(2,1)}, bf16[256,2048]{1,0:T(8,128)(2,1)}, u32[]{:S(2)}, u32[]{:S(2)}) collective-permute-start(bf16[256,2048]{1,0:T(8,128)(2,1)} %get-tuple-element.204), channel_id=1, source_target_pairs={{0,16},{1,9},{2,18},{3,11},{4,20},{5,13},{6,22},{7,15},{8,24},{9,1... | collective-permute-start | bytes 3145736 | tf_op jit(solution)/shard_map/ppermute | solution.py:88
  287.7 26.6 %collective-permute-start.31 = (bf16[960,512]{1,0:T(8,128)(2,1)S(1)}, bf16[960,512]{1,0:T(8,128)(2,1)S(1)}, u32[]{:S(2)}, u32[]{:S(2)}) collective-permute-start(bf16[960,512]{1,0:T(8,128)(2,1)S(1)} %copy-done.47), channel_id=1, source_target_pairs={{0,1},{1,0},{2,3},{3,2},{4,5},{5,4},{6,7},{7,6},{8,9},{9,8},{10,11... | collective-permute-start | bytes 2949128 | tf_op jit(solution)/shard_map/ppermute | solution.py:102
  298.4 27.2 %collective-permute-start.45 = (bf16[720,640]{1,0:T(8,128)(2,1)S(1)}, bf16[720,640]{1,0:T(8,128)(2,1)S(1)}, u32[]{:S(2)}, u32[]{:S(2)}) collective-permute-start(bf16[720,640]{1,0:T(8,128)(2,1)S(1)} %pad_maximum_fusion.2), channel_id=1, source_target_pairs={{0,4},{1,3},{2,6},{3,1},{4,0},{5,7},{6,2},{7,5},{8,12},{9,11},{10,... | collective-permute-start | bytes 2764808 | tf_op jit(solution)/shard_map/ppermute | solution.py:98
  300.6 11.3 %collective-permute-start.38 = (bf16[256,768]{1,0:T(8,128)(2,1)S(1)}, bf16[256,768]{1,0:T(8,128)(2,1)S(1)}, u32[]{:S(2)}, u32[]{:S(2)}) collective-permute-start(bf16[256,768]{1,0:T(8,128)(2,1)S(1)} %get-tuple-element.213), channel_id=1, source_target_pairs={{0,16},{1,9},{2,18},{3,11},{4,20},{5,13},{6,22},{7,15},{8,24},{9,1... | collective-permute-start | bytes 1179656 | tf_op jit(solution)/shard_map/ppermute | solution.py:88
  303.6 17.4 %collective-permute-start.33 = (bf16[128,2048]{1,0:T(8,128)(2,1)S(1)}, bf16[128,2048]{1,0:T(8,128)(2,1)S(1)}, u32[]{:S(2)}, u32[]{:S(2)}) collective-permute-start(bf16[128,2048]{1,0:T(8,128)(2,1)S(1)} %add_convert_fusion.9), channel_id=1, source_target_pairs={{0,8},{1,17},{2,10},{3,19},{4,12},{5,21},{6,14},{7,23},{8,0},{9,25... | collective-permute-start | bytes 1572872 | tf_op jit(solution)/shard_map/ppermute | solution.py:88
  312.0 6.0 %collective-permute-start.39 = (bf16[128,768]{1,0:T(8,128)(2,1)S(1)}, bf16[128,768]{1,0:T(8,128)(2,1)S(1)}, u32[]{:S(2)}, u32[]{:S(2)}) collective-permute-start(bf16[128,768]{1,0:T(8,128)(2,1)S(1)} %add_convert_fusion.16), channel_id=1, source_target_pairs={{0,8},{1,17},{2,10},{3,19},{4,12},{5,21},{6,14},{7,23},{8,0},{9,25... | collective-permute-start | bytes 589832 | tf_op jit(solution)/shard_map/ppermute | solution.py:88
  318.1 8.6 %collective-permute-start.40 = (bf16[128,768]{1,0:T(8,128)(2,1)S(1)}, bf16[128,768]{1,0:T(8,128)(2,1)S(1)}, u32[]{:S(2)}, u32[]{:S(2)}) collective-permute-start(bf16[128,768]{1,0:T(8,128)(2,1)S(1)} %add_convert_fusion.15), channel_id=1, source_target_pairs={{0,2},{1,5},{2,0},{3,7},{4,6},{5,1},{6,4},{7,3},{8,10},{9,13},{10,... | collective-permute-start | bytes 589832 | tf_op jit(solution)/shard_map/ppermute | solution.py:98
  322.4 20.3 %collective-permute-start.34 = (bf16[128,2048]{1,0:T(8,128)(2,1)S(1)}, bf16[128,2048]{1,0:T(8,128)(2,1)S(1)}, u32[]{:S(2)}, u32[]{:S(2)}) collective-permute-start(bf16[128,2048]{1,0:T(8,128)(2,1)S(1)} %add_convert_fusion.8), channel_id=1, source_target_pairs={{0,2},{1,5},{2,0},{3,7},{4,6},{5,1},{6,4},{7,3},{8,10},{9,13},{10,... | collective-permute-start | bytes 1572872 | tf_op jit(solution)/shard_map/ppermute | solution.py:98
  326.7 16.4 %collective-permute-start.41 = (bf16[128,768]{1,0:T(8,128)(2,1)S(1)}, bf16[128,768]{1,0:T(8,128)(2,1)S(1)}, u32[]{:S(2)}, u32[]{:S(2)}) collective-permute-start(bf16[128,768]{1,0:T(8,128)(2,1)S(1)} %add_convert_fusion.14), channel_id=1, source_target_pairs={{0,4},{1,3},{2,6},{3,1},{4,0},{5,7},{6,2},{7,5},{8,12},{9,11},{10,... | collective-permute-start | bytes 589832 | tf_op jit(solution)/shard_map/ppermute | solution.py:98
  342.8 15.2 %collective-permute-start.35 = (bf16[128,2048]{1,0:T(8,128)(2,1)S(1)}, bf16[128,2048]{1,0:T(8,128)(2,1)S(1)}, u32[]{:S(2)}, u32[]{:S(2)}) collective-permute-start(bf16[128,2048]{1,0:T(8,128)(2,1)S(1)} %add_convert_fusion.7), channel_id=1, source_target_pairs={{0,4},{1,3},{2,6},{3,1},{4,0},{5,7},{6,2},{7,5},{8,12},{9,11},{10,... | collective-permute-start | bytes 1572872 | tf_op jit(solution)/shard_map/ppermute | solution.py:98
  343.1 20.9 %collective-permute-start.46 = (bf16[1440,640]{1,0:T(8,128)(2,1)S(1)}, bf16[1440,640]{1,0:T(8,128)(2,1)S(1)}, u32[]{:S(2)}, u32[]{:S(2)}) collective-permute-start(bf16[1440,640]{1,0:T(8,128)(2,1)S(1)} %pad_maximum_fusion), channel_id=1, source_target_pairs={{0,1},{1,0},{2,3},{3,2},{4,5},{5,4},{6,7},{7,6},{8,9},{9,8},{10,11... | collective-permute-start | bytes 5529608 | tf_op jit(solution)/shard_map/ppermute | solution.py:102
  343.2 15.0 %collective-permute-start.42 = (bf16[128,768]{1,0:T(8,128)(2,1)S(1)}, bf16[128,768]{1,0:T(8,128)(2,1)S(1)}, u32[]{:S(2)}, u32[]{:S(2)}) collective-permute-start(bf16[128,768]{1,0:T(8,128)(2,1)S(1)} %add_convert_fusion.13), channel_id=1, source_target_pairs={{0,1},{1,0},{2,3},{3,2},{4,5},{5,4},{6,7},{7,6},{8,9},{9,8},{10,11... | collective-permute-start | bytes 589832 | tf_op jit(solution)/shard_map/ppermute | solution.py:102
  358.2 2.0 collective-permute-start.36
  (54 other events, 363.7 us)
where the time goes:
time: 375 us; the launch traced here: 370 us
  Pallas kernels  151 us (40%)
  waiting for transfers between devices  129 us (34%)
  starting transfers between devices  43.9 us (12%)
  other arithmetic  22.4 us (6%)
  local copies, waits for them, and re-layouts  22.3 us (6%)
    pallas_call x16, Pallas kernels, call(): pl.pallas_call(kernel, out_shape=tuple((jax.ShapeDtypeStruct(s, d) for s,...  151 us
    ppermute x14, waiting for transfers between devices, hop_z(): return lax.ppermute(after(x, *self.gates), ('dp', 'ctx'), perm)  89.7 us
    ppermute x12, waiting for transfers between devices, hop_d(): return lax.ppermute(after(x, *self.gates), ('dp', 'ctx'), perm)  25.1 us
    ppermute x12, starting transfers between devices, hop_d(): return lax.ppermute(after(x, *self.gates), ('dp', 'ctx'), perm)  21.2 us
    unnamed x108, local copies, waits for them, and re-layouts  18.7 us
    ppermute x14, starting transfers between devices, hop_z(): return lax.ppermute(after(x, *self.gates), ('dp', 'ctx'), perm)  17.9 us
    convert_element_type x14, other arithmetic, add(): functools.reduce(lambda a, b: a + b, [t.astype(F32) for t in terms])  15.1 us
    ppermute x21, waiting for transfers between devices, swap(): return lax.ppermute(after(x, *self.gates), ('dp', 'ctx'), perm)  14 us
  transfers between devices with their start and end apart: 47, of which 28 were waited for; matrix products, arithmetic and copies ran while one was open for 6% of the time, Pallas kernels for 26%

commit v1 on v0

--- a/solution.py
+++ b/solution.py
@@ -126,7 +126,7 @@
         for j in range(self.kz):
             got = self.hop_z(x, j)
             yield got
-            x = add(x, got)
+            x = add(x, after(got, *self.gates))
         return x
 
     def owners(self):
@@ -760,6 +760,19 @@
             down_t[:, at : at + quarter] = block.T
 
 
+def final_kernel(q_low, q_high, k_low, k_high, qkv, out, mlp_gain, attn_gain):
+    skip = 2 * q_low.shape[0] - qkv.shape[0]
+    model = out.shape[1]
+    low = model // 128 * 128
+    q = jnp.concatenate([q_low[...].astype(F32), q_high[...].astype(F32)[skip:]], axis=0)
+    k = jnp.concatenate([k_low[...].astype(F32), k_high[...].astype(F32)[skip:]], axis=0)
+    out[...] = q[:, :model]
+    qkv[:, 0:QW] = q[:, model + 128 : model + 128 + QW]
+    qkv[:, QW:] = k[:, 0 : 2 * KW]
+    mlp_gain[...] = q[:, low : low + 128].T[model - low : model - low + 1]
+    attn_gain[...] = k[:, 2 * KW :].T[0:1]
+
+
 def local(
     nd, nc, tokens, positions, w_qkv, w_out, w_gate, w_up, w_down, g_attn, g_mlp, grad_out
 ):
@@ -974,36 +987,44 @@
     out_got = plan.swap(sums[1])
     output = (mid + (sums[0].astype(F32) + out_got.astype(F32))).astype(BF16)
     kv_total = Task(plan.reduce_all(*both_cores(*parts), small=True))
-    kv_halves = kv_total.finish()
-    query_halves = query_total.finish()
+    packs = list(pack_total.finish())
     gate, up, down = call(
         functools.partial(unpack_kernel, nd),
         "unpack",
         [(w.shape, F32) for w in (w_gate, w_up, w_down.T)],
-        list(pack_total.finish()),
+        packs,
         limit=24,
         us=6,
     )
-
-    def whole(halves):
-        low, high = halves
-        return jnp.concatenate([low, high[2 * take - shard :]], axis=0).astype(F32)
-
-    query_whole = whole(query_halves)
-    kv_whole = whole(kv_halves)
-    qkv_whole = jnp.concatenate(
-        [query_whole[:, model + 128 : 2 * model + 128], kv_whole[:, : 2 * KW]], axis=1
+    kv_total.go(plan.kd + plan.kz)
+    query_total.go(plan.kd - 1 + plan.kz)
+    plan.gates = (up,)
+    kv_halves = kv_total.finish()
+    query_halves = query_total.finish()
+
+    qkv_whole, out_whole, mlp_gain, attn_gain = call(
+        final_kernel,
+        "final",
+        [
+            ((shard, width), F32),
+            ((shard, model), F32),
+            ((1, shard), F32),
+            ((1, shard), F32),
+        ],
+        list(query_halves) + list(kv_halves),
+        limit=12,
+        us=2,
     )
     return (
         output.T[None],
         grad_tokens.T[None],
         qkv_whole,
-        query_whole[:, :model],
+        out_whole,
         gate,
         up,
         down.T,
-        kv_whole[:, 2 * KW],
-        query_whole[:, model],
+        attn_gain[0],
+        mlp_gain[0],
     )
 
 

time: 375 us -> 372 us (level)
    ppermute x14, waiting for transfers between devices: 89.7 us -> 93.5 us  [hop_z(): return lax.ppermute(after(x, *self.gates), ('dp', 'ctx'), perm)]
    unnamed x108 -> x104, local copies, waits for them, and re-layouts: 18.7 us -> 17.8 us
    pallas_call x16 -> x17, Pallas kernels: 151 us -> 151 us  [call(): pl.pallas_call(kernel, out_shape=tuple((jax.ShapeDtypeStruct(s, d) for s,...]
  transfers between devices with their start and end apart: 47 -> 47, of which waited for: 28 -> 26; matrix products, arithmetic and copies ran while one was open for 6% -> 5% of each run, Pallas kernels for 26% -> 27%
where the time goes in v1:
time: 372 us; the launch traced here: 367 us
  Pallas kernels  151 us (41%)
  waiting for transfers between devices  129 us (35%)
  starting transfers between devices  45.6 us (12%)
  local copies, waits for them, and re-layouts  20 us (5%)
  other arithmetic  19.3 us (5%)
    pallas_call x17, Pallas kernels, call(): pl.pallas_call(kernel, out_shape=tuple((jax.ShapeDtypeStruct(s, d) for s,...  151 us
    ppermute x14, waiting for transfers between devices, hop_z(): return lax.ppermute(after(x, *self.gates), ('dp', 'ctx'), perm)  93.5 us
    ppermute x12, waiting for transfers between devices, hop_d(): return lax.ppermute(after(x, *self.gates), ('dp', 'ctx'), perm)  23.2 us
    ppermute x12, starting transfers between devices, hop_d(): return lax.ppermute(after(x, *self.gates), ('dp', 'ctx'), perm)  20.9 us
    ppermute x14, starting transfers between devices, hop_z(): return lax.ppermute(after(x, *self.gates), ('dp', 'ctx'), perm)  20 us
    unnamed x104, local copies, waits for them, and re-layouts  17.8 us
    convert_element_type x14, other arithmetic, add(): functools.reduce(lambda a, b: a + b, [t.astype(F32) for t in terms])  15.1 us
    ppermute x21, waiting for transfers between devices, swap(): return lax.ppermute(after(x, *self.gates), ('dp', 'ctx'), perm)  12.8 us
  transfers between devices with their start and end apart: 47, of which 26 were waited for; matrix products, arithmetic and copies ran while one was open for 5% of the time, Pallas kernels for 27%

profile of v1, /device:TPU:0, one launch (start us, length us, event | category | flops | bytes accessed | tf_op | source)
XLA Modules:
  0.0 367.4 jit_solution(15845461299289277024)
XLA Ops:
  2.4 2.7 collective-permute-start.1
  14.7 2.8 collective-permute-start.3
  17.9 5.8 %collective-permute-done.3.refs_3_ = bf16[128,1664]{1,0:T(8,128)(2,1)S(1)} collective-permute-done((bf16[128,1664]{1,0:T(8,128)(2,1)}, bf16[128,1664]{1,0:T(8,128)(2,1)S(1)}, u32[]{:S(2)}, u32[]{:S(2)}) %collective-permute-start.3) | collective-permute-done | bytes 426016 | tf_op jit(solution)/shard_map/ppermute | solution.py:88
  23.7 1.9 collective-permute-start.11
  25.7 1.8 collective-permute-start.12
  30.2 5.2 %project.1 = (bf16[960,512]{1,0:T(8,128)(2,1)S(1)}, bf16[960,512]{1,0:T(8,128)(2,1)S(1)}, bf16[656,512]{1,0:T(8,128)(2,1)}, bf16[960,1664]{1,0:T(8,128)(2,1)S(1)}, bf16[960,128]{1,0:T(8,128)(2,1)S(1)}) custom-call(s32[9]{0:T(128)S(1)} %pad_add_fusion.idx, s32[1,512]{1,0:T(1,128)S(1)} %copy-done.45, f32[32,512]{1,0:T(8,128)S(1)} %get-tuple-element.260.cos, ...), custom_call_target="tpu_custom_call" | custom-call | flops 60000000 | tf_op jit(solution)/shard_map/project/pallas_call | solution.py:38
  38.2 2.6 collective-permute-start.10
  42.5 8.7 %attention_forward.4 = (f32[16,512]{1,0:T(8,128)S(1)}, f32[16,512]{1,0:T(8,128)S(1)}, f32[960,512]{1,0:T(8,128)S(1)}) custom-call(s32[2]{0:T(128)S(1)} %and_select_fusion.q_blocks, bf16[960,512]{1,0:T(8,128)(2,1)S(1)} %get-tuple-element.163.qT.refs_0_, bf16[656,512]{1,0:T(8,128)(2,1)} %get-tuple-element.133.refs_0_.refs_6_, ...), custom_call_target="tpu_custom_call" | custom-call | flops 80000000 | tf_op jit(solution)/shard_map/attention_forward/pallas_call | solution.py:38
  51.2 19.2 %collective-permute-done.10.refs_0_.refs_6_ = bf16[656,512]{1,0:T(8,128)(2,1)} collective-permute-done((bf16[656,512]{1,0:T(8,128)(2,1)}, bf16[656,512]{1,0:T(8,128)(2,1)}, u32[]{:S(2)}, u32[]{:S(2)}) %collective-permute-start.10) | collective-permute-done | bytes 671776 | tf_op jit(solution)/shard_map/ppermute | solution.py:98
  70.4 5.0 %collective-permute-done.11.refs_1_ = bf16[1800,640]{1,0:T(8,128)(2,1)} collective-permute-done((bf16[1800,640]{1,0:T(8,128)(2,1)S(1)}, bf16[1800,640]{1,0:T(8,128)(2,1)}, u32[]{:S(2)}, u32[]{:S(2)}) %collective-permute-start.11) | collective-permute-done | bytes 2304032 | tf_op jit(solution)/shard_map/ppermute | solution.py:88
  77.0 2.1 collective-permute-start.13
  79.8 7.6 %attention_forward.5 = (f32[16,512]{1,0:T(8,128)S(1)}, f32[16,512]{1,0:T(8,128)S(1)}, f32[960,512]{1,0:T(8,128)S(1)}) custom-call(s32[2]{0:T(128)S(1)} %and_select_fusion.q_blocks, bf16[960,512]{1,0:T(8,128)(2,1)S(1)} %get-tuple-element.163.qT.refs_0_, bf16[656,512]{1,0:T(8,128)(2,1)} %collective-permute-done.9.refs_0_.refs_6_, ...), custom_call_target="tpu_custom_call" | custom-call | flops 80000000 | tf_op jit(solution)/shard_map/attention_forward/pallas_call | solution.py:38
  87.4 7.9 %attention_forward.6 = (f32[16,512]{1,0:T(8,128)S(1)}, f32[16,512]{1,0:T(8,128)S(1)}, f32[960,512]{1,0:T(8,128)S(1)}) custom-call(s32[2]{0:T(128)S(1)} %and_select_fusion.q_blocks, bf16[960,512]{1,0:T(8,128)(2,1)S(1)} %get-tuple-element.163.qT.refs_0_, bf16[656,512]{1,0:T(8,128)(2,1)} %collective-permute-done.10.refs_0_.refs_6_, ...), custom_call_target="tpu_custom_call" | custom-call | flops 80000000 | tf_op jit(solution)/shard_map/attention_forward/pallas_call | solution.py:38
  96.0 2.1 collective-permute-done.16.refs_1_
  98.2 7.1 %attention_forward.7 = (bf16[960,512]{1,0:T(8,128)(2,1)S(1)}, f32[16,512]{1,0:T(8,128)S(1)}) custom-call(s32[2]{0:T(128)S(1)} %and_select_fusion.q_blocks, bf16[960,512]{1,0:T(8,128)(2,1)S(1)} %get-tuple-element.163.qT.refs_0_, bf16[656,512]{1,0:T(8,128)(2,1)S(1)} %collective-permute-done.13.refs_0_.refs_6_, ...), custom_call_target="tpu_custom_call" | custom-call | flops 80000000 | tf_op jit(solution)/shard_map/attention_forward/pallas_call | solution.py:38
  105.4 5.6 %middle.1 = (f32[960,512]{1,0:T(8,128)S(1)}, bf16[960,512]{1,0:T(8,128)(2,1)S(1)}, bf16[960,960]{1,0:T(8,128)(2,1)S(1)}) custom-call(s32[9]{0:T(128)S(1)} %pad_add_fusion.idx, bf16[960,512]{1,0:T(8,128)(2,1)S(1)} %bitcast.28, bf16[960,512]{1,0:T(8,128)(2,1)S(1)} %get-tuple-element.156.oT, bf16[960,128]{1,0:T(8,128)(2,1)S(1)} %get-tuple-element.132.gain_ref, ...), custom_call_target="tpu_custom_call" | custom-call | flops 50000000 | tf_op jit(solution)/shard_map/middle/pallas_call | solution.py:38
  111.2 2.4 collective-permute-done.18.n_sib
  113.7 43.2 %mlp.1 = (bf16[960,512]{1,0:T(8,128)(2,1)S(1)}, bf16[960,512]{1,0:T(8,128)(2,1)S(1)}, bf16[960,512]{1,0:T(8,128)(2,1)S(1)}, bf16[960,512]{1,0:T(8,128)(2,1)S(1)}...) custom-call(s32[9]{0:T(128)S(1)} %pad_add_fusion.idx, bf16[960,512]{1,0:T(8,128)(2,1)S(1)} %get-tuple-element.160.n_own, ...), custom_call_target="tpu_custom_call" | custom-call | flops 360000000 | tf_op jit(solution)/shard_map/mlp/pallas_call | solution.py:38
  159.5 2.2 collective-permute-done.20.gn_got
  161.7 3.0 turn.1
  171.4 9.7 %attention_backward.4 = (f32[2,960,512]{2,1,0:T(8,128)S(1)}, bf16[640,512]{1,0:T(8,128)(2,1)S(1)}) custom-call(s32[4]{0:T(128)S(1)} %pad_add_fusion.1.q_blocks, bf16[960,512]{1,0:T(8,128)(2,1)S(1)} %get-tuple-element.163.qT.refs_0_, bf16[960,512]{1,0:T(8,128)(2,1)S(1)} %collective-permute-done.19.refs_1_, bf16[960,512]{1,0:T(8,128)(2,1)S(1)} %get-tuple-element.169.refs_2_, ...), custom_call_target="tpu_custom_call" | custom-call | flops 100000000 | tf_op jit(solution)/shard_map/attention_backward/pallas_call | solution.py:38
  181.1 1.8 collective-permute-start.23
  182.9 10.9 %attention_backward.5 = (f32[2,960,512]{2,1,0:T(8,128)S(1)}, bf16[640,512]{1,0:T(8,128)(2,1)}) custom-call(s32[4]{0:T(128)S(1)} %pad_add_fusion.1.q_blocks, bf16[960,512]{1,0:T(8,128)(2,1)S(1)} %get-tuple-element.163.qT.refs_0_, bf16[960,512]{1,0:T(8,128)(2,1)S(1)} %collective-permute-done.19.refs_1_, bf16[960,512]{1,0:T(8,128)(2,1)S(1)} %get-tuple-element.169.refs_2_, ...), custom_call_target="tpu_custom_call" | custom-call | flops 100000000 | tf_op jit(solution)/shard_map/attention_backward/pallas_call | solution.py:38
  193.9 5.8 %collective-permute-done.23.refs_7_ = bf16[640,512]{1,0:T(8,128)(2,1)S(1)} collective-permute-done((bf16[640,512]{1,0:T(8,128)(2,1)S(1)}, bf16[640,512]{1,0:T(8,128)(2,1)S(1)}, u32[]{:S(2)}, u32[]{:S(2)}) %collective-permute-start.23) | collective-permute-done | bytes 655392 | tf_op jit(solution)/shard_map/ppermute | solution.py:98
  201.2 3.2 add_convert_fusion.1
  204.4 1.8 collective-permute-start.25
  207.7 2.1 copy-done.11
  210.9 9.9 %attention_backward.6 = (f32[2,960,512]{2,1,0:T(8,128)S(1)}, bf16[640,512]{1,0:T(8,128)(2,1)S(1)}) custom-call(s32[4]{0:T(128)S(1)} %pad_add_fusion.1.q_blocks, bf16[960,512]{1,0:T(8,128)(2,1)S(1)} %get-tuple-element.163.qT.refs_0_, bf16[960,512]{1,0:T(8,128)(2,1)S(1)} %collective-permute-done.19.refs_1_, bf16[960,512]{1,0:T(8,128)(2,1)S(1)} %get-tuple-element.169.refs_2_, ...), custom_call_target="tpu_custom_call" | custom-call | flops 100000000 | tf_op jit(solution)/shard_map/attention_backward/pallas_call | solution.py:38
  220.8 4.3 %collective-permute-done.26.refs_0_ = bf16[640,512]{1,0:T(8,128)(2,1)} collective-permute-done((bf16[640,512]{1,0:T(8,128)(2,1)}, bf16[640,512]{1,0:T(8,128)(2,1)}, u32[]{:S(2)}, u32[]{:S(2)}) %collective-permute-start.26) | collective-permute-done | bytes 655392 | tf_op jit(solution)/shard_map/ppermute | solution.py:98
  225.1 3.0 collective-permute-done.25
  228.6 11.8 %attention_backward.7 = (f32[960,512]{1,0:T(8,128)S(1)}, bf16[960,512]{1,0:T(8,128)(2,1)S(1)}, bf16[640,512]{1,0:T(8,128)(2,1)S(1)}) custom-call(s32[4]{0:T(128)S(1)} %pad_add_fusion.1.q_blocks, bf16[960,512]{1,0:T(8,128)(2,1)S(1)} %get-tuple-element.163.qT.refs_0_, bf16[960,512]{1,0:T(8,128)(2,1)S(1)} %collective-permute-done.19.refs_1_, ...), custom_call_target="tpu_custom_call" | custom-call | flops 100000000 | tf_op jit(solution)/shard_map/attention_backward/pallas_call | solution.py:38
  240.5 3.0 add_convert_fusion
  247.7 6.9 %query.1 = (bf16[960,512]{1,0:T(8,128)(2,1)S(1)}, bf16[512,2048]{1,0:T(8,128)(2,1)S(1)}, bf16[512,2048]{1,0:T(8,128)(2,1)}) custom-call(s32[9]{0:T(128)S(1)} %pad_add_fusion.idx, f32[960,512]{1,0:T(8,128)S(1)} %get-tuple-element.190.dq, bf16[960,512]{1,0:T(8,128)(2,1)S(1)} %collective-permute-done.28.dq_got, f32[32,512]{1,0:T(8,128)S(1)} %copy-done.29, ...), custom_call_target="tpu_custom_call" | custom-call | flops 40000000 | tf_op jit(solution)/shard_map/query/pallas_call | solution.py:38
  255.5 13.6 %collective-permute-done.29 = bf16[720,640]{1,0:T(8,128)(2,1)} collective-permute-done((bf16[720,640]{1,0:T(8,128)(2,1)S(1)}, bf16[720,640]{1,0:T(8,128)(2,1)}, u32[]{:S(2)}, u32[]{:S(2)}) %collective-permute-start.29) | collective-permute-done | bytes 921632 | tf_op jit(solution)/shard_map/ppermute | solution.py:98
  269.1 1.8 add_convert_fusion.5
  273.6 3.6 add_convert_fusion.2
  277.3 5.6 %last.1 = (bf16[960,512]{1,0:T(8,128)(2,1)}, bf16[512,768]{1,0:T(8,128)(2,1)S(1)}, bf16[512,768]{1,0:T(8,128)(2,1)S(1)}) custom-call(s32[9]{0:T(128)S(1)} %pad_add_fusion.idx, bf16[960,512]{1,0:T(8,128)(2,1)S(1)} %bitcast.29, bf16[960,128]{1,0:T(8,128)(2,1)S(1)} %get-tuple-element.132.gain_ref, f32[32,512]{1,0:T(8,128)S(1)} %copy-done.29, ...), custom_call_target="tpu_custom_call" | custom-call | flops 60000000 | tf_op jit(solution)/shard_map/last/pallas_call | solution.py:38
  286.2 11.6 %collective-permute-done.37 = bf16[360,640]{1,0:T(8,128)(2,1)S(1)} collective-permute-done((bf16[360,640]{1,0:T(8,128)(2,1)S(1)}, bf16[360,640]{1,0:T(8,128)(2,1)S(1)}, u32[]{:S(2)}, u32[]{:S(2)}) %collective-permute-start.37) | collective-permute-done | bytes 460832 | tf_op jit(solution)/shard_map/ppermute | solution.py:98
  298.0 1.8 collective-permute-start.38
  302.7 1.8 collective-permute-start.33
  304.5 6.9 %collective-permute-done.42 = bf16[256,768]{1,0:T(8,128)(2,1)S(1)} collective-permute-done((bf16[256,768]{1,0:T(8,128)(2,1)S(1)}, bf16[256,768]{1,0:T(8,128)(2,1)S(1)}, u32[]{:S(2)}, u32[]{:S(2)}) %collective-permute-start.42) | collective-permute-done | bytes 393248 | tf_op jit(solution)/shard_map/ppermute | solution.py:88
  311.4 2.4 collective-permute-start.43
  313.8 8.5 %collective-permute-done.38 = bf16[720,640]{1,0:T(8,128)(2,1)S(1)} collective-permute-done((bf16[720,640]{1,0:T(8,128)(2,1)S(1)}, bf16[720,640]{1,0:T(8,128)(2,1)S(1)}, u32[]{:S(2)}, u32[]{:S(2)}) %collective-permute-start.38) | collective-permute-done | bytes 921632 | tf_op jit(solution)/shard_map/ppermute | solution.py:98
  324.7 2.0 collective-permute-start.44
  327.5 15.7 %collective-permute-done.44 = bf16[128,768]{1,0:T(8,128)(2,1)S(1)} collective-permute-done((bf16[128,768]{1,0:T(8,128)(2,1)S(1)}, bf16[128,768]{1,0:T(8,128)(2,1)S(1)}, u32[]{:S(2)}, u32[]{:S(2)}) %collective-permute-start.44) | collective-permute-done | bytes 196640 | tf_op jit(solution)/shard_map/ppermute | solution.py:98
  347.2 5.0 %unpack.1 = (f32[240,2560]{1,0:T(8,128)}, f32[240,2560]{1,0:T(8,128)}, f32[960,640]{1,0:T(8,128)}) custom-call(bf16[1440,640]{1,0:T(8,128)(2,1)S(1)} %get-tuple-element.248.pack_0, bf16[1440,640]{1,0:T(8,128)(2,1)S(1)} %get-tuple-element.247.pack_1), custom_call_target="tpu_custom_call" | custom-call | flops 60000000 | tf_op jit(solution)/shard_map/unpack/pallas_call | solution.py:38
  352.3 10.9 %collective-permute-done.35 = bf16[128,2048]{1,0:T(8,128)(2,1)S(1)} collective-permute-done((bf16[128,2048]{1,0:T(8,128)(2,1)S(1)}, bf16[128,2048]{1,0:T(8,128)(2,1)S(1)}, u32[]{:S(2)}, u32[]{:S(2)}) %collective-permute-start.35) | collective-permute-done | bytes 524320 | tf_op jit(solution)/shard_map/ppermute | solution.py:98
  365.4 1.8 final.1
  (207 shorter events, 59.7 us)
Async XLA Ops:
  0.7 23.1 %collective-permute-start = (bf16[960,512]{1,0:T(8,128)(2,1)}, bf16[960,512]{1,0:T(8,128)(2,1)}, u32[]{:S(2)}, u32[]{:S(2)}) collective-permute-start(bf16[960,512]{1,0:T(8,128)(2,1)} %bitcast.30), channel_id=1, source_target_pairs={{0,1},{1,0},{2,3},{3,2},{4,5},{5,4},{6,7},{7,6},{8,9},{9,8},{10,11... | collective-permute-start | bytes 2949128 | tf_op jit(solution)/shard_map/ppermute | solution.py:102
  2.4 12.2 %collective-permute-start.1 = (bf16[128,1664]{1,0:T(8,128)(2,1)S(1)}, bf16[128,1664]{1,0:T(8,128)(2,1)}, u32[]{:S(2)}, u32[]{:S(2)}) collective-permute-start(bf16[128,1664]{1,0:T(8,128)(2,1)S(1)} %concatenate.16.refs_0_), channel_id=1, source_target_pairs={{0,8},{1,17},{2,10},{3,19},{4,12},{5,21},{6,14},{7,23},{8,0},{9,25... | collective-permute-start | bytes 1277960 | tf_op jit(solution)/shard_map/ppermute | solution.py:88
  5.1 12.3 %collective-permute-start.2 = (bf16[128,1664]{1,0:T(8,128)(2,1)S(1)}, bf16[128,1664]{1,0:T(8,128)(2,1)}, u32[]{:S(2)}, u32[]{:S(2)}) collective-permute-start(bf16[128,1664]{1,0:T(8,128)(2,1)S(1)} %concatenate.16.refs_0_), channel_id=1, source_target_pairs={{0,16},{1,9},{2,18},{3,11},{4,20},{5,13},{6,22},{7,15},{8,24},{9,1... | collective-permute-start | bytes 1277960 | tf_op jit(solution)/shard_map/ppermute | solution.py:88
  6.6 11.3 %collective-permute-start.4 = (bf16[128,1664]{1,0:T(8,128)(2,1)S(1)}, bf16[128,1664]{1,0:T(8,128)(2,1)}, u32[]{:S(2)}, u32[]{:S(2)}) collective-permute-start(bf16[128,1664]{1,0:T(8,128)(2,1)S(1)} %concatenate.16.refs_0_), channel_id=1, source_target_pairs={{0,1},{1,0},{2,3},{3,2},{4,5},{5,4},{6,7},{7,6},{8,9},{9,8},{10,11... | collective-permute-start | bytes 1277960 | tf_op jit(solution)/shard_map/ppermute | solution.py:102
  14.7 9.1 %collective-permute-start.3 = (bf16[128,1664]{1,0:T(8,128)(2,1)}, bf16[128,1664]{1,0:T(8,128)(2,1)S(1)}, u32[]{:S(2)}, u32[]{:S(2)}) collective-permute-start(bf16[128,1664]{1,0:T(8,128)(2,1)} %collective-permute-done.1.refs_1_), channel_id=1, source_target_pairs={{0,16},{1,9},{2,18},{3,11},{4,20},{5,13},{6,22},{7,15},{8,24},{9,1... | collective-permute-start | bytes 1277960 | tf_op jit(solution)/shard_map/ppermute | solution.py:88
  17.4 6.3 %collective-permute-start.5 = (bf16[128,1664]{1,0:T(8,128)(2,1)}, bf16[128,1664]{1,0:T(8,128)(2,1)S(1)}, u32[]{:S(2)}, u32[]{:S(2)}) collective-permute-start(bf16[128,1664]{1,0:T(8,128)(2,1)} %collective-permute-done.1.refs_1_), channel_id=1, source_target_pairs={{0,1},{1,0},{2,3},{3,2},{4,5},{5,4},{6,7},{7,6},{8,9},{9,8},{10,11... | collective-permute-start | bytes 1277960 | tf_op jit(solution)/shard_map/ppermute | solution.py:102
  17.4 6.3 %collective-permute-start.6 = (bf16[128,1664]{1,0:T(8,128)(2,1)}, bf16[128,1664]{1,0:T(8,128)(2,1)S(1)}, u32[]{:S(2)}, u32[]{:S(2)}) collective-permute-start(bf16[128,1664]{1,0:T(8,128)(2,1)} %collective-permute-done.2.refs_2_), channel_id=1, source_target_pairs={{0,1},{1,0},{2,3},{3,2},{4,5},{5,4},{6,7},{7,6},{8,9},{9,8},{10,11... | collective-permute-start | bytes 1277960 | tf_op jit(solution)/shard_map/ppermute | solution.py:102
  23.7 51.7 %collective-permute-start.11 = (bf16[1800,640]{1,0:T(8,128)(2,1)S(1)}, bf16[1800,640]{1,0:T(8,128)(2,1)}, u32[]{:S(2)}, u32[]{:S(2)}) collective-permute-start(bf16[1800,640]{1,0:T(8,128)(2,1)S(1)} %pack.1.refs_0_), channel_id=1, source_target_pairs={{0,8},{1,17},{2,10},{3,19},{4,12},{5,21},{6,14},{7,23},{8,0},{9,25... | collective-permute-start | bytes 6912008 | tf_op jit(solution)/shard_map/ppermute | solution.py:88
  25.7 49.8 %collective-permute-start.12 = (bf16[1800,640]{1,0:T(8,128)(2,1)S(1)}, bf16[1800,640]{1,0:T(8,128)(2,1)}, u32[]{:S(2)}, u32[]{:S(2)}) collective-permute-start(bf16[1800,640]{1,0:T(8,128)(2,1)S(1)} %pack.1.refs_0_), channel_id=1, source_target_pairs={{0,16},{1,9},{2,18},{3,11},{4,20},{5,13},{6,22},{7,15},{8,24},{9,1... | collective-permute-start | bytes 6912008 | tf_op jit(solution)/shard_map/ppermute | solution.py:88
  27.5 1.8 collective-permute-start.7
  38.1 4.4 %collective-permute-start.8 = (bf16[656,512]{1,0:T(8,128)(2,1)}, bf16[656,512]{1,0:T(8,128)(2,1)}, u32[]{:S(2)}, u32[]{:S(2)}) collective-permute-start(bf16[656,512]{1,0:T(8,128)(2,1)} %get-tuple-element.133.refs_0_.refs_6_), channel_id=1, source_target_pairs={{0,1},{1,0},{2,3},{3,2},{4,5},{5,4},{6,7},{7,6},{8,9},{9,8},{10,11... | collective-permute-start | bytes 2015240 | tf_op jit(solution)/shard_map/ppermute | solution.py:102
  38.2 32.2 %collective-permute-start.10 = (bf16[656,512]{1,0:T(8,128)(2,1)}, bf16[656,512]{1,0:T(8,128)(2,1)}, u32[]{:S(2)}, u32[]{:S(2)}) collective-permute-start(bf16[656,512]{1,0:T(8,128)(2,1)} %get-tuple-element.133.refs_0_.refs_6_), channel_id=1, source_target_pairs={{0,4},{1,3},{2,6},{3,1},{4,0},{5,7},{6,2},{7,5},{8,12},{9,11},{10,... | collective-permute-start | bytes 2015240 | tf_op jit(solution)/shard_map/ppermute | solution.py:98
  40.8 29.6 %collective-permute-start.9 = (bf16[656,512]{1,0:T(8,128)(2,1)}, bf16[656,512]{1,0:T(8,128)(2,1)}, u32[]{:S(2)}, u32[]{:S(2)}) collective-permute-start(bf16[656,512]{1,0:T(8,128)(2,1)} %get-tuple-element.133.refs_0_.refs_6_), channel_id=1, source_target_pairs={{0,2},{1,5},{2,0},{3,7},{4,6},{5,1},{6,4},{7,3},{8,10},{9,13},{10,... | collective-permute-start | bytes 2015240 | tf_op jit(solution)/shard_map/ppermute | solution.py:98
  75.4 29.9 %collective-permute-start.17 = (bf16[1800,640]{1,0:T(8,128)(2,1)}, bf16[1800,640]{1,0:T(8,128)(2,1)S(1)}, u32[]{:S(2)}, u32[]{:S(2)}) collective-permute-start(bf16[1800,640]{1,0:T(8,128)(2,1)} %collective-permute-done.11.refs_1_), channel_id=1, source_target_pairs={{0,16},{1,9},{2,18},{3,11},{4,20},{5,13},{6,22},{7,15},{8,24},{9,1... | collective-permute-start | bytes 6912008 | tf_op jit(solution)/shard_map/ppermute | solution.py:88
  76.5 2.6 collective-permute-start.14
  76.5 3.3 collective-permute-start.15
  77.0 19.1 %collective-permute-start.13 = (bf16[656,512]{1,0:T(8,128)(2,1)}, bf16[656,512]{1,0:T(8,128)(2,1)S(1)}, u32[]{:S(2)}, u32[]{:S(2)}) collective-permute-start(bf16[656,512]{1,0:T(8,128)(2,1)} %collective-permute-done.9.refs_0_.refs_6_), channel_id=1, source_target_pairs={{0,4},{1,3},{2,6},{3,1},{4,0},{5,7},{6,2},{7,5},{8,12},{9,11},{10,... | collective-permute-start | bytes 2015240 | tf_op jit(solution)/shard_map/ppermute | solution.py:98
  96.0 2.1 collective-permute-start.16
  105.3 56.4 %copy-start.3 = (bf16[960,512]{1,0:T(8,128)(2,1)}, bf16[960,512]{1,0:T(8,128)(2,1)S(1)}, u32[]{:S(2)}) copy-start(bf16[960,512]{1,0:T(8,128)(2,1)S(1)} %get-tuple-element.156.oT) | copy-start | bytes 2949124
  111.0 2.6 collective-permute-start.18
  157.8 43.4 %collective-permute-start.24 = (bf16[2880,640]{1,0:T(8,128)(2,1)}, bf16[2880,640]{1,0:T(8,128)(2,1)}, u32[]{:S(2)}, u32[]{:S(2)}) collective-permute-start(bf16[2880,640]{1,0:T(8,128)(2,1)} %get-tuple-element.175), channel_id=1, source_target_pairs={{0,16},{1,9},{2,18},{3,11},{4,20},{5,13},{6,22},{7,15},{8,24},{9,1... | collective-permute-start | bytes 11059208 | tf_op jit(solution)/shard_map/ppermute | solution.py:88
  158.2 3.5 collective-permute-start.20
  159.5 9.5 %collective-permute-start.19 = (bf16[960,512]{1,0:T(8,128)(2,1)S(1)}, bf16[960,512]{1,0:T(8,128)(2,1)S(1)}, u32[]{:S(2)}, u32[]{:S(2)}) collective-permute-start(bf16[960,512]{1,0:T(8,128)(2,1)S(1)} %get-tuple-element.163.qT.refs_0_), channel_id=1, source_target_pairs={{0,1},{1,0},{2,3},{3,2},{4,5},{5,4},{6,7},{7,6},{8,9},{9,8},{10,11... | collective-permute-start | bytes 2949128 | tf_op jit(solution)/shard_map/ppermute | solution.py:102
  167.6 2.7 collective-permute-start.21
  168.8 1.5 collective-permute-start.22
  181.1 18.6 %collective-permute-start.23 = (bf16[640,512]{1,0:T(8,128)(2,1)S(1)}, bf16[640,512]{1,0:T(8,128)(2,1)S(1)}, u32[]{:S(2)}, u32[]{:S(2)}) collective-permute-start(bf16[640,512]{1,0:T(8,128)(2,1)S(1)} %get-tuple-element.171), channel_id=1, source_target_pairs={{0,4},{1,3},{2,6},{3,1},{4,0},{5,7},{6,2},{7,5},{8,12},{9,11},{10,... | collective-permute-start | bytes 1966088 | tf_op jit(solution)/shard_map/ppermute | solution.py:98
  204.4 23.6 %collective-permute-start.25 = (bf16[1440,640]{1,0:T(8,128)(2,1)}, bf16[1440,640]{1,0:T(8,128)(2,1)}, u32[]{:S(2)}, u32[]{:S(2)}) collective-permute-start(bf16[1440,640]{1,0:T(8,128)(2,1)} %add_convert_fusion.1), channel_id=1, source_target_pairs={{0,8},{1,17},{2,10},{3,19},{4,12},{5,21},{6,14},{7,23},{8,0},{9,25... | collective-permute-start | bytes 5529608 | tf_op jit(solution)/shard_map/ppermute | solution.py:88
  206.2 18.8 %collective-permute-start.26 = (bf16[640,512]{1,0:T(8,128)(2,1)}, bf16[640,512]{1,0:T(8,128)(2,1)}, u32[]{:S(2)}, u32[]{:S(2)}) collective-permute-start(bf16[640,512]{1,0:T(8,128)(2,1)} %get-tuple-element.183), channel_id=1, source_target_pairs={{0,4},{1,3},{2,6},{3,1},{4,0},{5,7},{6,2},{7,5},{8,12},{9,11},{10,... | collective-permute-start | bytes 1966088 | tf_op jit(solution)/shard_map/ppermute | solution.py:98
  228.1 17.0 %collective-permute-start.27 = (bf16[640,512]{1,0:T(8,128)(2,1)S(1)}, bf16[640,512]{1,0:T(8,128)(2,1)S(1)}, u32[]{:S(2)}, u32[]{:S(2)}) collective-permute-start(bf16[640,512]{1,0:T(8,128)(2,1)S(1)} %get-tuple-element.189), channel_id=1, source_target_pairs={{0,2},{1,5},{2,0},{3,7},{4,6},{5,1},{6,4},{7,3},{8,10},{9,13},{10,... | collective-permute-start | bytes 1966088 | tf_op jit(solution)/shard_map/ppermute | solution.py:98
  245.1 2.6 collective-permute-start.28
  245.2 23.9 %collective-permute-start.29 = (bf16[720,640]{1,0:T(8,128)(2,1)S(1)}, bf16[720,640]{1,0:T(8,128)(2,1)}, u32[]{:S(2)}, u32[]{:S(2)}) collective-permute-start(bf16[720,640]{1,0:T(8,128)(2,1)S(1)} %constant_dynamic-slice_fusion.1), channel_id=1, source_target_pairs={{0,4},{1,3},{2,6},{3,1},{4,0},{5,7},{6,2},{7,5},{8,12},{9,11},{10,... | collective-permute-start | bytes 2764808 | tf_op jit(solution)/shard_map/ppermute | solution.py:98
  269.1 4.5 %collective-permute-start.30 = (bf16[512,2048]{1,0:T(8,128)(2,1)}, bf16[512,2048]{1,0:T(8,128)(2,1)}, u32[]{:S(2)}, u32[]{:S(2)}) collective-permute-start(bf16[512,2048]{1,0:T(8,128)(2,1)} %get-tuple-element.204), channel_id=1, source_target_pairs={{0,1},{1,0},{2,3},{3,2},{4,5},{5,4},{6,7},{7,6},{8,9},{9,8},{10,11... | collective-permute-start | bytes 6291464 | tf_op jit(solution)/shard_map/ppermute | solution.py:102
  271.0 13.5 %collective-permute-start.36 = (bf16[360,640]{1,0:T(8,128)(2,1)S(1)}, bf16[360,640]{1,0:T(8,128)(2,1)S(1)}, u32[]{:S(2)}, u32[]{:S(2)}) collective-permute-start(bf16[360,640]{1,0:T(8,128)(2,1)S(1)} %constant_dynamic-slice_fusion), channel_id=1, source_target_pairs={{0,2},{1,5},{2,0},{3,7},{4,6},{5,1},{6,4},{7,3},{8,10},{9,13},{10,... | collective-permute-start | bytes 1382408 | tf_op jit(solution)/shard_map/ppermute | solution.py:98
  284.6 13.1 %collective-permute-start.37 = (bf16[360,640]{1,0:T(8,128)(2,1)S(1)}, bf16[360,640]{1,0:T(8,128)(2,1)S(1)}, u32[]{:S(2)}, u32[]{:S(2)}) collective-permute-start(bf16[360,640]{1,0:T(8,128)(2,1)S(1)} %add_convert_fusion.10), channel_id=1, source_target_pairs={{0,2},{1,5},{2,0},{3,7},{4,6},{5,1},{6,4},{7,3},{8,10},{9,13},{10,... | collective-permute-start | bytes 1382408 | tf_op jit(solution)/shard_map/ppermute | solution.py:98
  284.7 15.1 %collective-permute-start.41 = (bf16[512,768]{1,0:T(8,128)(2,1)S(1)}, bf16[512,768]{1,0:T(8,128)(2,1)S(1)}, u32[]{:S(2)}, u32[]{:S(2)}) collective-permute-start(bf16[512,768]{1,0:T(8,128)(2,1)S(1)} %get-tuple-element.229), channel_id=1, source_target_pairs={{0,1},{1,0},{2,3},{3,2},{4,5},{5,4},{6,7},{7,6},{8,9},{9,8},{10,11... | collective-permute-start | bytes 2359304 | tf_op jit(solution)/shard_map/ppermute | solution.py:102
  284.8 16.7 %collective-permute-start.32 = (bf16[256,2048]{1,0:T(8,128)(2,1)}, bf16[256,2048]{1,0:T(8,128)(2,1)}, u32[]{:S(2)}, u32[]{:S(2)}) collective-permute-start(bf16[256,2048]{1,0:T(8,128)(2,1)} %get-tuple-element.212), channel_id=1, source_target_pairs={{0,16},{1,9},{2,18},{3,11},{4,20},{5,13},{6,22},{7,15},{8,24},{9,1... | collective-permute-start | bytes 3145736 | tf_op jit(solution)/shard_map/ppermute | solution.py:88
  298.0 24.3 %collective-permute-start.38 = (bf16[720,640]{1,0:T(8,128)(2,1)S(1)}, bf16[720,640]{1,0:T(8,128)(2,1)S(1)}, u32[]{:S(2)}, u32[]{:S(2)}) collective-permute-start(bf16[720,640]{1,0:T(8,128)(2,1)S(1)} %pad_maximum_fusion.1), channel_id=1, source_target_pairs={{0,4},{1,3},{2,6},{3,1},{4,0},{5,7},{6,2},{7,5},{8,12},{9,11},{10,... | collective-permute-start | bytes 2764808 | tf_op jit(solution)/shard_map/ppermute | solution.py:98
  300.0 11.4 %collective-permute-start.42 = (bf16[256,768]{1,0:T(8,128)(2,1)S(1)}, bf16[256,768]{1,0:T(8,128)(2,1)S(1)}, u32[]{:S(2)}, u32[]{:S(2)}) collective-permute-start(bf16[256,768]{1,0:T(8,128)(2,1)S(1)} %get-tuple-element.230), channel_id=1, source_target_pairs={{0,16},{1,9},{2,18},{3,11},{4,20},{5,13},{6,22},{7,15},{8,24},{9,1... | collective-permute-start | bytes 1179656 | tf_op jit(solution)/shard_map/ppermute | solution.py:88
  302.7 20.2 %collective-permute-start.33 = (bf16[128,2048]{1,0:T(8,128)(2,1)S(1)}, bf16[128,2048]{1,0:T(8,128)(2,1)S(1)}, u32[]{:S(2)}, u32[]{:S(2)}) collective-permute-start(bf16[128,2048]{1,0:T(8,128)(2,1)S(1)} %add_convert_fusion.9), channel_id=1, source_target_pairs={{0,8},{1,17},{2,10},{3,19},{4,12},{5,21},{6,14},{7,23},{8,0},{9,25... | collective-permute-start | bytes 1572872 | tf_op jit(solution)/shard_map/ppermute | solution.py:88
  311.4 11.5 %collective-permute-start.43 = (bf16[128,768]{1,0:T(8,128)(2,1)S(1)}, bf16[128,768]{1,0:T(8,128)(2,1)S(1)}, u32[]{:S(2)}, u32[]{:S(2)}) collective-permute-start(bf16[128,768]{1,0:T(8,128)(2,1)S(1)} %add_convert_fusion.16), channel_id=1, source_target_pairs={{0,8},{1,17},{2,10},{3,19},{4,12},{5,21},{6,14},{7,23},{8,0},{9,25... | collective-permute-start | bytes 589832 | tf_op jit(solution)/shard_map/ppermute | solution.py:88
  322.8 23.6 %collective-permute-start.39 = (bf16[1440,640]{1,0:T(8,128)(2,1)S(1)}, bf16[1440,640]{1,0:T(8,128)(2,1)S(1)}, u32[]{:S(2)}, u32[]{:S(2)}) collective-permute-start(bf16[1440,640]{1,0:T(8,128)(2,1)S(1)} %pad_maximum_fusion), channel_id=1, source_target_pairs={{0,1},{1,0},{2,3},{3,2},{4,5},{5,4},{6,7},{7,6},{8,9},{9,8},{10,11... | collective-permute-start | bytes 5529608 | tf_op jit(solution)/shard_map/ppermute | solution.py:102
  324.5 20.3 %collective-permute-start.34 = (bf16[128,2048]{1,0:T(8,128)(2,1)S(1)}, bf16[128,2048]{1,0:T(8,128)(2,1)S(1)}, u32[]{:S(2)}, u32[]{:S(2)}) collective-permute-start(bf16[128,2048]{1,0:T(8,128)(2,1)S(1)} %add_convert_fusion.8), channel_id=1, source_target_pairs={{0,2},{1,5},{2,0},{3,7},{4,6},{5,1},{6,4},{7,3},{8,10},{9,13},{10,... | collective-permute-start | bytes 1572872 | tf_op jit(solution)/shard_map/ppermute | solution.py:98
  324.7 18.5 %collective-permute-start.44 = (bf16[128,768]{1,0:T(8,128)(2,1)S(1)}, bf16[128,768]{1,0:T(8,128)(2,1)S(1)}, u32[]{:S(2)}, u32[]{:S(2)}) collective-permute-start(bf16[128,768]{1,0:T(8,128)(2,1)S(1)} %add_convert_fusion.15), channel_id=1, source_target_pairs={{0,2},{1,5},{2,0},{3,7},{4,6},{5,1},{6,4},{7,3},{8,10},{9,13},{10,... | collective-permute-start | bytes 589832 | tf_op jit(solution)/shard_map/ppermute | solution.py:98
  326.7 36.7 %collective-permute-start.31 = (bf16[960,512]{1,0:T(8,128)(2,1)S(1)}, bf16[960,512]{1,0:T(8,128)(2,1)S(1)}, u32[]{:S(2)}, u32[]{:S(2)}) collective-permute-start(bf16[960,512]{1,0:T(8,128)(2,1)S(1)} %copy-done.47), channel_id=1, source_target_pairs={{0,1},{1,0},{2,3},{3,2},{4,5},{5,4},{6,7},{7,6},{8,9},{9,8},{10,11... | collective-permute-start | bytes 2949128 | tf_op jit(solution)/shard_map/ppermute | solution.py:102
  343.2 9.0 %collective-permute-start.45 = (bf16[128,768]{1,0:T(8,128)(2,1)S(1)}, bf16[128,768]{1,0:T(8,128)(2,1)S(1)}, u32[]{:S(2)}, u32[]{:S(2)}) collective-permute-start(bf16[128,768]{1,0:T(8,128)(2,1)S(1)} %add_convert_fusion.14), channel_id=1, source_target_pairs={{0,4},{1,3},{2,6},{3,1},{4,0},{5,7},{6,2},{7,5},{8,12},{9,11},{10,... | collective-permute-start | bytes 589832 | tf_op jit(solution)/shard_map/ppermute | solution.py:98
  345.0 18.2 %collective-permute-start.35 = (bf16[128,2048]{1,0:T(8,128)(2,1)S(1)}, bf16[128,2048]{1,0:T(8,128)(2,1)S(1)}, u32[]{:S(2)}, u32[]{:S(2)}) collective-permute-start(bf16[128,2048]{1,0:T(8,128)(2,1)S(1)} %add_convert_fusion.7), channel_id=1, source_target_pairs={{0,4},{1,3},{2,6},{3,1},{4,0},{5,7},{6,2},{7,5},{8,12},{9,11},{10,... | collective-permute-start | bytes 1572872 | tf_op jit(solution)/shard_map/ppermute | solution.py:98
  352.2 12.7 %collective-permute-start.46 = (bf16[128,768]{1,0:T(8,128)(2,1)S(1)}, bf16[128,768]{1,0:T(8,128)(2,1)S(1)}, u32[]{:S(2)}, u32[]{:S(2)}) collective-permute-start(bf16[128,768]{1,0:T(8,128)(2,1)S(1)} %add_convert_fusion.13), channel_id=1, source_target_pairs={{0,1},{1,0},{2,3},{3,2},{4,5},{5,4},{6,7},{7,6},{8,9},{9,8},{10,11... | collective-permute-start | bytes 589832 | tf_op jit(solution)/shard_map/ppermute | solution.py:102
  363.3 2.0 collective-permute-start.40
  (51 other events, 344.5 us)
